TPU v7x, 32 devices: a whole 2x2x4 slice. The times are simulated.
32 devices in a mesh: grp: 4 (over y, x), tm: 8 (over z, core).
Axes of the slice: x: 2, y: 2, z: 4, core: 2. Of those that a mesh axis runs over, the one named last changes fastest.
Arguments:
- frames: float32 [32768, 768], P(('grp', 'tm')), may hold values from -6 to 6
- targets: float32 [32768, 256], P(('grp', 'tm')), may hold values from -6 to 6
- lengths: int32 [32, 3], P(('grp', 'tm')), may hold values from 1 to 512, 1024 in all within a row
- span_starts: int32 [32768], P(('grp', 'tm')), may hold values from 0 to 1, as said below
- distractors: int32 [32768, 100], P(('grp', 'tm')), may hold values from 0 to 1023
- w_query: float32 [768, 768], replicated, may hold values from -0.21875 to 0.21875
- b_query: float32 [768], replicated, may hold values from -2 to 2
- w_key: float32 [768, 768], replicated, may hold values from -0.21875 to 0.21875
- w_value: float32 [768, 768], replicated, may hold values from -0.21875 to 0.21875
- b_value: float32 [768], replicated, may hold values from -2 to 2
- w_out: float32 [768, 768], replicated, may hold values from -1.75 to 1.75
- b_out: float32 [768], replicated, may hold values from -2 to 2
- norm_gain: float32 [768], replicated, may hold values from 0.5 to 1.5
- norm_bias: float32 [768], replicated, may hold values from -2 to 2
- w_up: float32 [768, 3072], replicated, may hold values from -0.21875 to 0.21875
- b_up: float32 [3072], replicated, may hold values from -2 to 2
- w_down: float32 [3072, 768], replicated, may hold values from -0.109375 to 0.109375
- b_down: float32 [768], replicated, may hold values from -2 to 2
- final_gain: float32 [768], replicated, may hold values from 0.5 to 1.5
- final_bias: float32 [768], replicated, may hold values from -2 to 2
- w_final: float32 [768, 256], replicated, may hold values from -0.21875 to 0.21875
- b_final: float32 [256], replicated, may hold values from -2 to 2
- w_target: float32 [256, 256], replicated, may hold values from -0.375 to 0.375
- b_target: float32 [256], replicated, may hold values from -2 to 2
Outputs:
- frame_loss: float32 [32768], P(('grp', 'tm'))
- input_grad: float32 [32768, 768], P(('grp', 'tm'))
- target_grad: float32 [32768, 256], P(('grp', 'tm'))
- grad_w_query: float32 [768, 768], P('tm')
- grad_b_query: float32 [768], P('tm')
- grad_w_key: float32 [768, 768], P('tm')
- grad_w_value: float32 [768, 768], P('tm')
- grad_b_value: float32 [768], P('tm')
- grad_w_out: float32 [768, 768], P('tm')
- grad_b_out: float32 [768], P('tm')
- grad_norm_gain: float32 [768], P('tm')
- grad_norm_bias: float32 [768], P('tm')
- grad_w_up: float32 [768, 3072], P('tm')
- grad_b_up: float32 [3072], P('tm')
- grad_w_down: float32 [3072, 768], P('tm')
- grad_b_down: float32 [768], P('tm')
- grad_final_gain: float32 [768], P('tm')
- grad_final_bias: float32 [768], P('tm')
- grad_w_final: float32 [768, 256], P('tm')
- grad_b_final: float32 [256], P('tm')
- grad_w_target: float32 [256, 256], P('tm')
- grad_b_target: float32 [256], P('tm')
Inputs may be any that keep to these rules, and one draw needn't show every extreme that they name: Row i holds the lengths of the 3 utterances of device i, in order, summing to 1024. `span_starts`: 1 marks a frame where a masked span of 10 frames begins.
All inputs are finite; a program needn't handle non-finite values.
Results may differ from a plain program's by a relative error of at most 0.018.
The roundings to bfloat16 on the way count: a program that leaves them out, or rounds other values in their place, can miss the bound.
Values may be sent and summed in bfloat16 or wider, within the bound.
No kernel may reach another device: no remote copies, remote signals or barrier semaphores. Data moves between devices by JAX's collectives and lax.ppermute only.
A program may use at most 448 MiB of HBM per device.

v0:
```python
import jax
import jax.numpy as jnp
from jax import lax
from jax.sharding import PartitionSpec as P

H = 12
HD = 64
NEG = 100
SPAN = 10


norm_eps = 1e-05
cosine_eps = 1e-06
similarity_softening_factor = 0.1
masked_score = -1e30


def to_low(values):
    return values.astype(jnp.bfloat16)


def product(left, right):
    return jnp.dot(left, right, preferred_element_type=jnp.float32)


def product_left(left, right):
    return lax.dot_general(
        left, right, (((0,), (0,)), ((), ())), preferred_element_type=jnp.float32
    )


def product_right(left, right):
    return lax.dot_general(
        left, right, (((1,), (1,)), ((), ())), preferred_element_type=jnp.float32
    )


def column_sum(values):
    return jnp.sum(values.astype(jnp.float32), axis=0)


def exact_gelu(values):
    return jax.nn.gelu(values, approximate=False)


def layer_norm(values, gain, bias):
    center = values - jnp.mean(values, axis=-1, keepdims=True)
    scale = lax.rsqrt(jnp.mean(center * center, axis=-1, keepdims=True) + norm_eps)
    normed = center * scale
    return (normed * gain + bias, normed, scale)


def layer_norm_back(grad, normed, scale, gain):
    grad_normed = grad * gain
    inner = (
        grad_normed
        - jnp.mean(grad_normed, axis=-1, keepdims=True)
        - normed * jnp.mean(grad_normed * normed, axis=-1, keepdims=True)
    )
    return (inner * scale, jnp.sum(grad * normed, axis=0), jnp.sum(grad, axis=0))


def segment_ids(lengths_row, count):
    bounds = jnp.cumsum(lengths_row)
    position = jnp.arange(count, dtype=jnp.int32)
    return jnp.sum((position[:, None] >= bounds[None, :]).astype(jnp.int32), axis=1)


def span_mask(starts, segment, count):
    covered = jnp.zeros((count,), jnp.float32)
    for offset in range(SPAN):
        earlier = jnp.concatenate([jnp.zeros((offset,), jnp.int32), starts[: count - offset]])
        earlier_segment = jnp.concatenate(
            [jnp.full((offset,), -1, jnp.int32), segment[: count - offset]]
        )
        hit = jnp.where(earlier_segment == segment, earlier, 0).astype(jnp.float32)
        covered = jnp.maximum(covered, hit)
    return covered


def normalized_embeddings(values):
    return values * lax.rsqrt(jnp.sum(values * values, axis=-1, keepdims=True) + cosine_eps)


def head_loss(final, correct_quantized_goal, collected_sample_lines, masked):
    closing_heading_normal = normalized_embeddings(final)
    matching_similarity_score = (
        jnp.sum(closing_heading_normal * normalized_embeddings(correct_quantized_goal), axis=-1)
        / similarity_softening_factor
    )
    decoy_similarity_score = (
        jnp.einsum(
            "og,oqg->oq",
            closing_heading_normal,
            normalized_embeddings(collected_sample_lines),
            precision=lax.Precision.HIGHEST,
        )
        / similarity_softening_factor
    )
    logits = jnp.concatenate([matching_similarity_score[:, None], decoy_similarity_score], axis=1)
    return masked * (jax.nn.logsumexp(logits, axis=1) - matching_similarity_score)


def score_block(query_part, key_heads, segment_part, segment):
    scores = jnp.einsum(
        "qhd,khd->hqk", query_part, key_heads, preferred_element_type=jnp.float32
    ) * HD ** (-0.5)
    same = segment_part[:, None] == segment[None, :]
    return jnp.where(same[None], scores, masked_score)


def attend(query, key, value, segment, block):
    count = query.shape[0]
    query_heads = query.reshape(count, H, HD)
    key_heads = key.reshape(count, H, HD)
    value_heads = value.reshape(count, H, HD)

    def one_block(index):
        start = index * block
        query_part = lax.dynamic_slice_in_dim(query_heads, start, block, 0)
        segment_part = lax.dynamic_slice_in_dim(segment, start, block, 0)
        scores = score_block(query_part, key_heads, segment_part, segment)
        highest = jnp.max(scores, axis=-1, keepdims=True)
        raised = jnp.exp(scores - highest)
        total = jnp.sum(raised, axis=-1, keepdims=True)
        prob = raised / total
        result = jnp.einsum(
            "hqk,khd->qhd", to_low(prob), value_heads, preferred_element_type=jnp.float32
        )
        return (result.reshape(block, H * HD), (highest + jnp.log(total))[..., 0])

    results, log_total = lax.map(one_block, jnp.arange(count // block, dtype=jnp.int32))
    return (results.reshape(count, H * HD), log_total)


def attend_back(query, key, value, segment, block, log_total, grad_low):
    count = query.shape[0]
    query_heads = query.reshape(count, H, HD)
    key_heads = key.reshape(count, H, HD)
    value_heads = value.reshape(count, H, HD)
    grad_heads = grad_low.reshape(count, H, HD)

    def one_block(carry, inputs):
        grad_key, grad_value = carry
        index, log_part = inputs
        start = index * block
        query_part = lax.dynamic_slice_in_dim(query_heads, start, block, 0)
        segment_part = lax.dynamic_slice_in_dim(segment, start, block, 0)
        grad_part = lax.dynamic_slice_in_dim(grad_heads, start, block, 0)
        scores = score_block(query_part, key_heads, segment_part, segment)
        prob = jnp.exp(scores - log_part[..., None])
        grad_prob = jnp.einsum(
            "qhd,khd->hqk", grad_part, value_heads, preferred_element_type=jnp.float32
        )
        grad_scores = prob * (grad_prob - jnp.sum(grad_prob * prob, axis=-1, keepdims=True))
        scores_low = to_low(grad_scores)
        grad_query = jnp.einsum(
            "hqk,khd->qhd", scores_low, key_heads, preferred_element_type=jnp.float32
        ) * HD ** (-0.5)
        grad_key = grad_key + jnp.einsum(
            "hqk,qhd->khd", scores_low, query_part, preferred_element_type=jnp.float32
        ) * HD ** (-0.5)
        grad_value = grad_value + jnp.einsum(
            "hqk,qhd->khd", to_low(prob), grad_part, preferred_element_type=jnp.float32
        )
        return ((grad_key, grad_value), grad_query)

    empty = jnp.zeros((count, H, HD), jnp.float32)
    indices = jnp.arange(count // block, dtype=jnp.int32)
    (grad_key, grad_value), grad_query = lax.scan(one_block, (empty, empty), (indices, log_total))
    return (
        grad_query.reshape(count, H * HD),
        grad_key.reshape(count, H * HD),
        grad_value.reshape(count, H * HD),
    )


def head_all(final, correct_quantized_goal, collected_sample_lines, masked):
    count = final.shape[0]
    piece_rows = min(count, 128)

    def head_piece(index):
        start = index * piece_rows
        final_part = lax.dynamic_slice_in_dim(final, start, piece_rows, 0)
        positive_part = lax.dynamic_slice_in_dim(
            correct_quantized_goal, start, piece_rows, 0
        ).astype(jnp.float32)
        fetched_part = lax.dynamic_slice_in_dim(
            collected_sample_lines, start, piece_rows, 0
        ).astype(jnp.float32)
        masked_part = lax.dynamic_slice_in_dim(masked, start, piece_rows, 0)

        def local_loss(final_in, positive_in, fetched_in):
            return head_loss(final_in, positive_in, fetched_in, masked_part)

        loss, backward = jax.vjp(local_loss, final_part, positive_part, fetched_part)
        grads = backward(jnp.ones_like(loss))
        return (loss, grads[0], grads[1], to_low(grads[2]))

    losses, d_final, d_positive, d_fetched = lax.map(
        head_piece, jnp.arange(count // piece_rows, dtype=jnp.int32)
    )
    width = final.shape[1]
    return (
        losses.reshape(count),
        d_final.reshape(count, width),
        d_positive.reshape(count, width),
        d_fetched.reshape(count, collected_sample_lines.shape[1], width),
    )


def owner_sums(row_index, row_grads, count):
    slots = row_index.shape[0]
    piece = min(slots, 6400)
    width = row_grads.shape[1]
    columns = jnp.arange(count, dtype=jnp.int32)

    def add_piece(index, total):
        start = index * piece
        rows_part = lax.dynamic_slice_in_dim(row_index, start, piece, 0)
        grads_part = lax.dynamic_slice_in_dim(row_grads, start, piece, 0)
        selector = (rows_part[:, None] == columns[None, :]).astype(jnp.bfloat16)
        return total + product_left(selector, grads_part)

    return lax.fori_loop(0, slots // piece, add_piece, jnp.zeros((count, width), jnp.float32))


def on_device(
    frames,
    targets,
    lengths,
    span_starts,
    distractors,
    w_query,
    b_query,
    w_key,
    w_value,
    b_value,
    w_out,
    b_out,
    norm_gain,
    norm_bias,
    w_up,
    b_up,
    w_down,
    b_down,
    final_gain,
    final_bias,
    w_final,
    b_final,
    w_target,
    b_target,
):
    count = frames.shape[0]
    width = targets.shape[1]
    block = min(count, 512)
    segment = segment_ids(lengths[0], count)
    masked = span_mask(span_starts, segment, count)
    query_matrix = to_low(w_query)
    key_matrix = to_low(w_key)
    value_matrix = to_low(w_value)
    out_matrix = to_low(w_out)
    up_matrix = to_low(w_up)
    down_matrix = to_low(w_down)
    final_matrix = to_low(w_final)
    target_matrix = to_low(w_target)
    targets_low = to_low(targets)
    target_low = to_low(product(targets_low, target_matrix) + b_target)
    members = lax.axis_size("tm")
    row_flat = distractors.reshape(-1)
    quota = row_flat.shape[0] // members
    wanted = row_flat.reshape(quota, members)
    asked = lax.all_to_all(wanted, "tm", split_axis=1, concat_axis=1, tiled=True)
    answer = jnp.take(target_low, asked.reshape(-1), axis=0).reshape(quota, members, width)
    arrived = lax.all_to_all(answer, "tm", split_axis=1, concat_axis=1, tiled=True)
    collected_sample_lines = arrived.reshape(count, NEG, width)
    frames_low = to_low(frames)
    query = to_low(product(frames_low, query_matrix) + b_query)
    key = to_low(product(frames_low, key_matrix))
    value = to_low(product(frames_low, value_matrix) + b_value)
    attended, log_total = attend(query, key, value, segment, block)
    attended_low = to_low(attended)
    resid = frames + product(attended_low, out_matrix) + b_out
    hidden, normed_one, scale_one = layer_norm(resid, norm_gain, norm_bias)
    hidden_low = to_low(hidden)
    upper = product(hidden_low, up_matrix) + b_up
    activated, gelu_back = jax.vjp(exact_gelu, upper)
    active_low = to_low(activated)
    second = hidden + product(active_low, down_matrix) + b_down
    output, normed_two, scale_two = layer_norm(second, final_gain, final_bias)
    output_low = to_low(output)
    final = product(output_low, final_matrix) + b_final
    losses, d_final, d_positive, d_fetched = head_all(
        final, target_low, collected_sample_lines, masked
    )
    sent = d_fetched.reshape(quota, members, width)
    came = lax.all_to_all(sent, "tm", split_axis=1, concat_axis=1, tiled=True)
    d_owned = owner_sums(asked.reshape(-1), came.reshape(-1, width), count)
    d_target_low = to_low(d_positive + d_owned)
    grad_w_target = product_left(targets_low, d_target_low)
    grad_b_target = column_sum(d_target_low)
    target_grad = product_right(d_target_low, target_matrix)
    d_final_low = to_low(d_final)
    grad_w_final = product_left(output_low, d_final_low)
    grad_b_final = column_sum(d_final_low)
    d_output = product_right(d_final_low, final_matrix)
    d_second, grad_final_gain, grad_final_bias = layer_norm_back(
        d_output, normed_two, scale_two, final_gain
    )
    d_down_low = to_low(d_second)
    grad_w_down = product_left(active_low, d_down_low)
    grad_b_down = column_sum(d_down_low)
    d_active = product_right(d_down_low, down_matrix)
    d_upper_low = to_low(gelu_back(d_active)[0])
    grad_w_up = product_left(hidden_low, d_upper_low)
    grad_b_up = column_sum(d_upper_low)
    d_hidden = d_second + product_right(d_upper_low, up_matrix)
    d_resid, grad_norm_gain, grad_norm_bias = layer_norm_back(
        d_hidden, normed_one, scale_one, norm_gain
    )
    d_branch_low = to_low(d_resid)
    grad_w_out = product_left(attended_low, d_branch_low)
    grad_b_out = column_sum(d_branch_low)
    d_attended_low = to_low(product_right(d_branch_low, out_matrix))
    d_query, d_key, d_value = attend_back(
        query, key, value, segment, block, log_total, d_attended_low
    )
    d_query_low = to_low(d_query)
    d_key_low = to_low(d_key)
    d_value_low = to_low(d_value)
    grad_w_query = product_left(frames_low, d_query_low)
    grad_b_query = column_sum(d_query_low)
    grad_w_key = product_left(frames_low, d_key_low)
    grad_w_value = product_left(frames_low, d_value_low)
    grad_b_value = column_sum(d_value_low)
    input_grad = (
        d_resid
        + product_right(d_query_low, query_matrix)
        + product_right(d_key_low, key_matrix)
        + product_right(d_value_low, value_matrix)
    )
    reduced = (
        lax.psum_scatter(grad_w_query, "tm", scatter_dimension=0, tiled=True),
        lax.psum_scatter(grad_b_query, "tm", scatter_dimension=0, tiled=True),
        lax.psum_scatter(grad_w_key, "tm", scatter_dimension=0, tiled=True),
        lax.psum_scatter(grad_w_value, "tm", scatter_dimension=0, tiled=True),
        lax.psum_scatter(grad_b_value, "tm", scatter_dimension=0, tiled=True),
        lax.psum_scatter(grad_w_out, "tm", scatter_dimension=0, tiled=True),
        lax.psum_scatter(grad_b_out, "tm", scatter_dimension=0, tiled=True),
        lax.psum_scatter(grad_norm_gain, "tm", scatter_dimension=0, tiled=True),
        lax.psum_scatter(grad_norm_bias, "tm", scatter_dimension=0, tiled=True),
        lax.psum_scatter(grad_w_up, "tm", scatter_dimension=0, tiled=True),
        lax.psum_scatter(grad_b_up, "tm", scatter_dimension=0, tiled=True),
        lax.psum_scatter(grad_w_down, "tm", scatter_dimension=0, tiled=True),
        lax.psum_scatter(grad_b_down, "tm", scatter_dimension=0, tiled=True),
        lax.psum_scatter(grad_final_gain, "tm", scatter_dimension=0, tiled=True),
        lax.psum_scatter(grad_final_bias, "tm", scatter_dimension=0, tiled=True),
        lax.psum_scatter(grad_w_final, "tm", scatter_dimension=0, tiled=True),
        lax.psum_scatter(grad_b_final, "tm", scatter_dimension=0, tiled=True),
        lax.psum_scatter(grad_w_target, "tm", scatter_dimension=0, tiled=True),
        lax.psum_scatter(grad_b_target, "tm", scatter_dimension=0, tiled=True),
    )
    summed = (
        lax.psum(reduced[0].astype(jnp.bfloat16), "grp").astype(jnp.float32),
        lax.psum(reduced[1].astype(jnp.bfloat16), "grp").astype(jnp.float32),
        lax.psum(reduced[2].astype(jnp.bfloat16), "grp").astype(jnp.float32),
        lax.psum(reduced[3].astype(jnp.bfloat16), "grp").astype(jnp.float32),
        lax.psum(reduced[4].astype(jnp.bfloat16), "grp").astype(jnp.float32),
        lax.psum(reduced[5].astype(jnp.bfloat16), "grp").astype(jnp.float32),
        lax.psum(reduced[6].astype(jnp.bfloat16), "grp").astype(jnp.float32),
        lax.psum(reduced[7].astype(jnp.bfloat16), "grp").astype(jnp.float32),
        lax.psum(reduced[8].astype(jnp.bfloat16), "grp").astype(jnp.float32),
        lax.psum(reduced[9].astype(jnp.bfloat16), "grp").astype(jnp.float32),
        lax.psum(reduced[10].astype(jnp.bfloat16), "grp").astype(jnp.float32),
        lax.psum(reduced[11].astype(jnp.bfloat16), "grp").astype(jnp.float32),
        lax.psum(reduced[12].astype(jnp.bfloat16), "grp").astype(jnp.float32),
        lax.psum(reduced[13].astype(jnp.bfloat16), "grp").astype(jnp.float32),
        lax.psum(reduced[14].astype(jnp.bfloat16), "grp").astype(jnp.float32),
        lax.psum(reduced[15].astype(jnp.bfloat16), "grp").astype(jnp.float32),
        lax.psum(reduced[16].astype(jnp.bfloat16), "grp").astype(jnp.float32),
        lax.psum(reduced[17].astype(jnp.bfloat16), "grp").astype(jnp.float32),
        lax.psum(reduced[18].astype(jnp.bfloat16), "grp").astype(jnp.float32),
    )
    return (
        losses,
        input_grad,
        target_grad,
        summed[0],
        summed[1],
        summed[2],
        summed[3],
        summed[4],
        summed[5],
        summed[6],
        summed[7],
        summed[8],
        summed[9],
        summed[10],
        summed[11],
        summed[12],
        summed[13],
        summed[14],
        summed[15],
        summed[16],
        summed[17],
        summed[18],
    )


def solution(mesh):
    placed = (
        P(("grp", "tm"), None),
        P(("grp", "tm"), None),
        P(("grp", "tm"), None),
        P(("grp", "tm")),
        P(("grp", "tm"), None),
        P(),
        P(),
        P(),
        P(),
        P(),
        P(),
        P(),
        P(),
        P(),
        P(),
        P(),
        P(),
        P(),
        P(),
        P(),
        P(),
        P(),
        P(),
        P(),
    )
    return jax.shard_map(
        on_device,
        mesh=mesh,
        in_specs=placed,
        out_specs=(
            P(("grp", "tm")),
            P(("grp", "tm"), None),
            P(("grp", "tm"), None),
            P("tm", None),
            P("tm"),
            P("tm", None),
            P("tm", None),
            P("tm"),
            P("tm", None),
            P("tm"),
            P("tm"),
            P("tm"),
            P("tm", None),
            P("tm"),
            P("tm", None),
            P("tm"),
            P("tm"),
            P("tm"),
            P("tm", None),
            P("tm"),
            P("tm", None),
            P("tm"),
        ),
        check_vma=False,
    )
```

profile of v0, /device:TPU:0, one launch (start us, length us, event | category | flops | bytes accessed | tf_op | source)
XLA Modules:
  0.0 3949.6 jit_solution(6429862250613725004)
XLA Ops:
  48.1 402.3 %gather_fusion = bf16[102400,256]{1,0:T(8,128)(2,1)} fusion(bf16[1024,256]{1,0:T(8,128)(2,1)S(1)} %fusion.86, s32[102400]{0:T(1024)S(1)} %broadcast_clamp_fusion), kind=kCustom, calls=%fused_computation | custom fusion | bytes 105267200 | tf_op jit(solution)/shard_map/jit(_take)/gather | solution.py:274
  450.5 34.5 copy_select_fusion
  507.2 91.8 %while.57 = (s32[]{:T(128)}, bf16[2,512,768]{2,1,0:T(8,128)(2,1)}, f32[2,12,512]{2,1,0:T(8,128)S(1)}, s32[2]{0:T(128)S(1)}, s32[1024]{0:T(1024)S(1)}, /*index=5*...) while((s32[]{:T(128)}, bf16[2,512,768]{2,1,0:T(8,128)(2,1)}, ...), condition=%wide.region_5.6_spmd, body=%wide.region_2.5_spmd.sunk | while | flops 1686628352 | bytes 186354384 | solution.py:132
  605.2 38.7 multiply_convert_fusion.1
  655.1 966.7 %all-to-all-done.1 = bf16[12800,8,256]{2,0,1:T(8,128)(2,1)} async-done(((bf16[12800,8,256]{2,0,1:T(8,128)(2,1)}), bf16[12800,8,256]{2,0,1:T(8,128)(2,1)}, u32[]{:S(2)}, u32[]{:S(2)}) %all-to-all-start.1) | async-done | bytes 52428832 | tf_op jit(solution)/shard_map/all_to_all | solution.py:275
  1621.8 47.2 %copy.132 = bf16[12800,8,256]{2,1,0:T(8,128)(2,1)} copy(bf16[12800,8,256]{2,0,1:T(8,128)(2,1)} %all-to-all-done.1) | data formatting | bytes 104857600 | tf_op jit(solution)/shard_map/all_to_all | solution.py:275
  1669.0 64.6 %reshape.368 = bf16[1024,100,256]{2,1,0:T(8,128)(2,1)} reshape(bf16[12800,8,256]{2,1,0:T(8,128)(2,1)} %copy.132) | data formatting | bytes 104857600 | tf_op jit(solution)/shard_map/reshape | solution.py:276
  1733.6 370.4 %while.58 = (s32[]{:T(128)}, f32[8,128]{1,0:T(8,128)S(1)}, bf16[8,128,256]{2,1,0:T(8,128)(2,1)S(1)}, f32[8,128,256]{2,1,0:T(8,128)}, bf16[8,128,100,256]{3,2,1,0...) while((s32[]{:T(128)}, f32[8,128]{1,0:T(8,128)S(1)}, ...), condition=%wide.region_20.21_spmd, body=%wide.region_10.0_spmd.sunk | while | flops 138831616 | bytes 44108528 | solution.py:200
  2104.0 64.8 %reshape_reshape.4 = bf16[12800,8,256]{2,1,0:T(8,128)(2,1)} reshape(bf16[8,128,100,256]{3,2,1,0:T(8,128)(2,1)} %get-tuple-element.281) | data formatting | bytes 104857600 | tf_op jit(solution)/shard_map/reshape;reshape | solution.py:296
  2168.9 34.7 copy.140
  2262.8 171.7 %while.59 = (s32[]{:T(128)}, f32[1024,12,64]{0,2,1:T(8,128)}, f32[1024,12,64]{0,2,1:T(8,128)}, bf16[2,512,12,64]{1,3,2,0:T(8,128)(2,1)}, s32[2]{0:T(128)S(1)}, /...) while((s32[]{:T(128)}, f32[1024,12,64]{0,2,1:T(8,128)}, ...), condition=%wide.region_27.28_spmd.clone, body=%wide.region_25.27_spmd.clone.sunk | while | flops 4125747200 | bytes 213043952 | solution.py:170
  2294.5 21.2 multiply_convert_fusion.3
  2379.0 21.2 multiply_convert_fusion.3
  2511.3 25.2 reduce-scatter.25.cloned.1.call-done
  2538.3 118.4 %reduce-scatter.29.cloned.1.call-done = f32[96,768]{1,0:T(8,128)} async-done(((f32[768,768]{1,0:T(8,128)}), f32[96,768]{1,0:T(8,128)}) %reduce-scatter.29.cloned.1.call-update) | async-done | bytes 294928
  2658.5 97.7 %reduce-scatter.27.cloned.1.call-done = f32[96,768]{1,0:T(8,128)} async-done(((f32[768,768]{1,0:T(8,128)}), f32[96,768]{1,0:T(8,128)}) %reduce-scatter.27.cloned.1.call-update) | async-done | bytes 294928
  2758.0 75.9 %reduce-scatter.17.cloned.1.call-done = f32[96,768]{1,0:T(8,128)} async-done(((f32[768,768]{1,0:T(8,128)}), f32[96,768]{1,0:T(8,128)}) %reduce-scatter.17.cloned.1.call-update) | async-done | bytes 294928 | tf_op jit(solution)/shard_map/reduce_scatter | solution.py:348
  2835.5 434.6 %reduce-scatter.21.cloned.1.call-done = f32[384,768]{1,0:T(8,128)} async-done(((f32[3072,768]{1,0:T(8,128)}), f32[384,768]{1,0:T(8,128)}) %reduce-scatter.21.cloned.1.call-update) | async-done | bytes 1179664 | tf_op jit(solution)/shard_map/reduce_scatter | solution.py:354
  3272.3 188.4 %reduce-scatter.19.cloned.1.call-done = f32[96,3072]{1,0:T(8,128)} async-done(((f32[768,3072]{1,0:T(8,128)}), f32[96,3072]{1,0:T(8,128)}) %reduce-scatter.19.cloned.1.call-update) | async-done | bytes 1179664 | tf_op jit(solution)/shard_map/reduce_scatter | solution.py:352
  3463.0 149.9 %all-to-all-done.2 = bf16[12800,8,256]{2,0,1:T(8,128)(2,1)} async-done(((bf16[12800,8,256]{2,0,1:T(8,128)(2,1)}), bf16[12800,8,256]{2,0,1:T(8,128)(2,1)}, u32[]{:S(2)}, u32[]{:S(2)}) %all-to-all-start.2) | async-done | bytes 52428832 | tf_op jit(solution)/shard_map/all_to_all | solution.py:297
  3612.9 47.3 %copy.200 = bf16[12800,8,256]{2,1,0:T(8,128)(2,1)} copy(bf16[12800,8,256]{2,0,1:T(8,128)(2,1)} %all-to-all-done.2) | data formatting | bytes 104857600 | tf_op jit(solution)/shard_map/all_to_all | solution.py:297
  3660.3 164.3 %while.60 = (s32[]{:T(128)}, f32[1024,256]{1,0:T(8,128)S(1)}, s32[102400]{0:T(1024)S(1)}, bf16[102400,256]{1,0:T(8,128)(2,1)}, s32[]{:T(128)}, /*index=5*/s32[]{:T(128)}, s32[]{:T(128)}, s32[]{:T(128)}) while((s32[]{:T(128)}, f32[1024,256]{1,0:T(8,128)S(1)}, s32[102400]{0:T(1024)S(1)}, bf16[102400,256]{1,0:T(8,128)(2,1)}, ...), condition=%wide.region_29.30_spmd.clone, body=%wide.region_28.29_spmd.clone.sunk | while | flops 3362521088 | bytes 5450901 | solution.py:225
  3846.8 27.3 all-reduce.27
  3883.4 43.3 %all-reduce.33.cloned.1.call-done = (bf16[32,256]{0,1:T(8,128)(2,1)}, bf16[96]{0:T(256)(128)(2,1)}, bf16[96]{0:T(256)(128)(2,1)}, bf16[96]{0:T(256)(128)(2,1)}, ...) async-done(((bf16[32,256]{0,1:T(8,128)(2,1)}, ...) | async-done | bytes 67984 | tf_op jit(solution)/shard_map/psum | solution.py:381
  (623 shorter events, 1004.1 us)
Async XLA Ops:
  18.0 19.2 all-to-all-start
  484.9 1136.9 %all-to-all-start.1 = ((bf16[12800,8,256]{2,0,1:T(8,128)(2,1)}), bf16[12800,8,256]{2,0,1:T(8,128)(2,1)}, u32[]{:S(2)}, u32[]{:S(2)}) async-start(bf16[12800,8,256]{2,0,1:T(8,128)(2,1)} %copy_select_fusion), calls=%async_computation.1 | async-start | bytes 104857600 | tf_op jit(solution)/shard_map/all_to_all | solution.py:275
  507.2 91.9 %copy-start.85 = (f32[768]{0:T(1024)S(1)}, f32[768]{0:T(1024)}, u32[]{:S(2)}) copy-start(f32[768]{0:T(1024)} %param.43) | copy-start | bytes 9220
  599.1 53.0 %copy-start.29 = (s32[1024]{0:T(1024)}, s32[1024]{0:T(1024)S(1)}, u32[]{:S(2)}) copy-start(s32[1024]{0:T(1024)S(1)} %get-tuple-element.1044) | copy-start | bytes 12292
  1669.0 64.6 %copy-start.1 = (bf16[1024,256]{1,0:T(8,128)(2,1)S(1)}, bf16[1024,256]{1,0:T(8,128)(2,1)}, u32[]{:S(2)}) copy-start(bf16[1024,256]{1,0:T(8,128)(2,1)} %copy-done) | copy-start | bytes 1572868
  1669.0 64.6 %copy-start.21 = (bf16[8,128,256]{2,1,0:T(8,128)(2,1)S(1)}, bf16[8,128,256]{2,1,0:T(8,128)(2,1)}, u32[]{:S(2)}) copy-start(bf16[8,128,256]{2,1,0:T(8,128)(2,1)} %custom-call.8) | copy-start | bytes 1572868
  1669.0 64.6 %copy-start.89 = (f32[8,128]{1,0:T(8,128)S(1)}, f32[8,128]{1,0:T(8,128)}, u32[]{:S(2)}) copy-start(f32[8,128]{1,0:T(8,128)} %custom-call.7) | copy-start | bytes 12292
  2104.0 64.9 %copy-start.90 = (f32[8,128]{1,0:T(8,128)}, f32[8,128]{1,0:T(8,128)S(1)}, u32[]{:S(2)}) copy-start(f32[8,128]{1,0:T(8,128)S(1)} %get-tuple-element.274) | copy-start | bytes 12292
  2104.0 108.5 %copy-start.22 = (bf16[8,128,256]{2,1,0:T(8,128)(2,1)}, bf16[8,128,256]{2,1,0:T(8,128)(2,1)S(1)}, u32[]{:S(2)}) copy-start(bf16[8,128,256]{2,1,0:T(8,128)(2,1)S(1)} %get-tuple-element.275) | copy-start | bytes 1572868
  2203.6 1409.3 %all-to-all-start.2 = ((bf16[12800,8,256]{2,0,1:T(8,128)(2,1)}), bf16[12800,8,256]{2,0,1:T(8,128)(2,1)}, u32[]{:S(2)}, u32[]{:S(2)}) async-start(bf16[12800,8,256]{2,0,1:T(8,128)(2,1)} %copy.140), calls=%async_computation.2 | async-start | bytes 104857600 | tf_op jit(solution)/shard_map/all_to_all | solution.py:297
  2212.4 324.1 %reduce-scatter.25.cloned.1.call-start = ((), (), s32[]{:S(2)}) async-start(), calls=%async_computation.15 | async-start | bytes 2654208
  2445.2 211.5 %reduce-scatter.29.cloned.1.call-start = ((), (), s32[]{:S(2)}) async-start(), calls=%async_computation.17 | async-start | bytes 2654208
  2453.4 302.8 %reduce-scatter.27.cloned.1.call-start = ((), (), s32[]{:S(2)}) async-start(), calls=%async_computation.16 | async-start | bytes 2654208
  2461.5 372.4 %reduce-scatter.17.cloned.1.call-start = ((), (), s32[]{:S(2)}) async-start(), calls=%async_computation.11 | async-start | bytes 2654208 | tf_op jit(solution)/shard_map/reduce_scatter | solution.py:348
  2465.8 804.3 %reduce-scatter.21.cloned.1.call-start = ((), (), s32[]{:S(2)}) async-start(), calls=%async_computation.13 | async-start | bytes 10616832 | tf_op jit(solution)/shard_map/reduce_scatter | solution.py:354
  2476.4 984.4 %reduce-scatter.19.cloned.1.call-start = ((), (), s32[]{:S(2)}) async-start(), calls=%async_computation.12 | async-start | bytes 10616832 | tf_op jit(solution)/shard_map/reduce_scatter | solution.py:352
  2488.7 1348.8 %reduce-scatter.23.cloned.1.call-start = ((), (), s32[]{:S(2)}) async-start(), calls=%async_computation.14 | async-start | bytes 884736 | tf_op jit(solution)/shard_map/reduce_scatter | solution.py:358
  2491.7 1347.4 %all-reduce.35.cloned.1.call-start = ((), (), s32[]{:S(2)}) async-start(), calls=%async_computation.20 | async-start | bytes 3833856 | tf_op jit(solution)/shard_map/psum | solution.py:364
  3462.9 197.3 %copy-start.41 = (f32[1024,256]{1,0:T(8,128)S(1)}, f32[1024,256]{1,0:T(8,128)}, u32[]{:S(2)}) copy-start(f32[1024,256]{1,0:T(8,128)} %custom-call.2) | copy-start | bytes 3145732
  3462.9 417.7 %reduce-scatter.31.cloned.1.call-start = ((), (), s32[]{:S(2)}) async-start(), calls=%async_computation.18 | async-start | bytes 294912
  3660.3 164.3 %copy-start.40 = (f32[8,128,256]{2,1,0:T(8,128)S(1)}, f32[8,128,256]{2,1,0:T(8,128)}, u32[]{:S(2)}) copy-start(f32[8,128,256]{2,1,0:T(8,128)} %get-tuple-element.280) | copy-start | bytes 3145732
  3827.2 99.6 %all-reduce.33.cloned.1.call-start = ((), (), s32[]{:S(2)}) async-start(), calls=%async_computation.19 | async-start | bytes 241664 | tf_op jit(solution)/shard_map/psum | solution.py:381
  3836.2 45.9 %copy-start.20 = (bf16[1024,256]{1,0:T(8,128)(2,1)S(1)}, bf16[1024,256]{1,0:T(8,128)(2,1)}, u32[]{:S(2)}) copy-start(bf16[1024,256]{1,0:T(8,128)(2,1)} %copy-done.19) | copy-start | bytes 1572868
  3836.2 45.9 %copy-start.43 = (f32[256,256]{1,0:T(8,128)S(1)}, f32[256,256]{1,0:T(8,128)}, u32[]{:S(2)}) copy-start(f32[256,256]{1,0:T(8,128)} %param.54) | copy-start | bytes 786436
  (86 other events, 730.5 us)
Sparse Core Ops, SparseCore 0:
  2445.3 91.1 reduce-scatter.24
  2538.8 117.8 reduce-scatter.28
  2659.0 97.1 reduce-scatter.26
  2758.4 75.4 reduce-scatter.16
  2836.0 434.0 reduce-scatter.20
  3272.3 188.4 reduce-scatter.18
  3463.6 76.6 reduce-scatter.22
  3545.8 66.2 all-reduce.34
  3827.3 29.3 reduce-scatter.30
  3882.2 44.4 all-reduce.32
where the time goes:
time: 3960 us; the launch traced here: 3950 us
  waiting for transfers between devices  2110 us (53%)
  local copies, waits for them, and re-layouts  762 us (19%)
  matrix products  665 us (17%)
  other arithmetic  316 us (8%)
    all_to_all x1, waiting for transfers between devices, on_device(): lax.all_to_all(answer, 'tm', split_axis=1, concat_axis=1, tiled=True)  967 us
    reduce_scatter x1, waiting for transfers between devices, on_device(): lax.psum_scatter(grad_w_down, 'tm', scatter_dimension=0, tiled=True)  435 us
    gather x1, local copies, waits for them, and re-layouts, on_device(): jnp.take(target_low, asked.reshape(-1), axis=0)  402 us
    unnamed x14, waiting for transfers between devices  241 us
    dot_general x24, matrix products, product_left(): lax.dot_general(left, right, (((0,), (0,)), ((), ())), preferred_element_...  198 us
    reduce_scatter x1, waiting for transfers between devices, on_device(): lax.psum_scatter(grad_w_up, 'tm', scatter_dimension=0, tiled=True)  188 us
    dot_general x16, matrix products, head_loss(): jnp.einsum('og,oqg->oq', closing_heading_normal, normalized_embeddings(co...  186 us
    all_to_all x1, waiting for transfers between devices, on_device(): came = lax.all_to_all(sent, 'tm', split_axis=1, concat_axis=1, tiled=True)  150 us
  transfers between devices with their start and end apart: 13, of which 10 were waited for; matrix products, arithmetic and copies ran while one was open for 17% of the time, Pallas kernels for 0%

commit v1 on v0

v1 whole, which is shorter than its diff:
```python
import functools
import math

import jax
import jax.numpy as jnp
from jax import lax
from jax.experimental import pallas as pl
from jax.experimental.pallas import tpu as pltpu
from jax.sharding import PartitionSpec as P

H = 12
HD = 64
NEG = 100
SPAN = 10


norm_eps = 1e-05
cosine_eps = 1e-06
similarity_softening_factor = 0.1
log2e = 1.4426950408889634
PAIR = 2 * HD
COLUMNS = 256
NT = (((1,), (1,)), ((), ()))
TN = (((0,), (0,)), ((), ()))
small_cost = pl.CostEstimate(flops=1, bytes_accessed=1, transcendentals=0)


def to_low(values):
    return values.astype(jnp.bfloat16)


def product(left, right):
    return jnp.dot(left, right, preferred_element_type=jnp.float32)


def product_left(left, right):
    return lax.dot_general(
        left, right, (((0,), (0,)), ((), ())), preferred_element_type=jnp.float32
    )


def product_right(left, right):
    return lax.dot_general(
        left, right, (((1,), (1,)), ((), ())), preferred_element_type=jnp.float32
    )


def column_sum(values):
    return jnp.sum(values.astype(jnp.float32), axis=0)


def exact_gelu(values):
    return jax.nn.gelu(values, approximate=False)


def layer_norm(values, gain, bias):
    center = values - jnp.mean(values, axis=-1, keepdims=True)
    scale = lax.rsqrt(jnp.mean(center * center, axis=-1, keepdims=True) + norm_eps)
    normed = center * scale
    return (normed * gain + bias, normed, scale)


def layer_norm_back(grad, normed, scale, gain):
    grad_normed = grad * gain
    inner = (
        grad_normed
        - jnp.mean(grad_normed, axis=-1, keepdims=True)
        - normed * jnp.mean(grad_normed * normed, axis=-1, keepdims=True)
    )
    return (inner * scale, jnp.sum(grad * normed, axis=0), jnp.sum(grad, axis=0))


def segment_ids(lengths_row, count):
    bounds = jnp.cumsum(lengths_row)
    position = jnp.arange(count, dtype=jnp.int32)
    return jnp.sum((position[:, None] >= bounds[None, :]).astype(jnp.int32), axis=1)


def span_mask(starts, segment, count):
    covered = jnp.zeros((count,), jnp.float32)
    for offset in range(SPAN):
        earlier = jnp.concatenate([jnp.zeros((offset,), jnp.int32), starts[: count - offset]])
        earlier_segment = jnp.concatenate(
            [jnp.full((offset,), -1, jnp.int32), segment[: count - offset]]
        )
        hit = jnp.where(earlier_segment == segment, earlier, 0).astype(jnp.float32)
        covered = jnp.maximum(covered, hit)
    return covered


def dot(a, b, dims=(((1,), (0,)), ((), ()))):
    return lax.dot_general(a, b, dims, preferred_element_type=jnp.float32)

def first_half(rows):
    return lax.broadcasted_iota(jnp.int32, (rows, PAIR), 1) < HD

def windows(span_ref, block, chunk, count, body):
    i = pl.program_id(0)
    start, chunks = span_ref[0, i], span_ref[1, i]
    total = count // chunk
    sizes = [s for s in range(2, total + 1)]
    for s in sizes:
        hit = (chunks <= s) if s == sizes[0] else (chunks == s)
        @pl.when(hit)
        def _(s=s):
            at = pl.multiple_of(jnp.minimum(start, total - s) * chunk, chunk)
            body(at, s * chunk)

def forward_kernel(pairs, chunk, unroll, span_ref, q_ref, k_ref, v_ref, hotq_ref, hotk_ref, *refs):
    casts = (len(refs) - 2) // 2
    out_ref, log_ref = refs[casts : casts + 2]
    for wide_ref, low_ref in zip(refs[:casts], refs[casts + 2 :]):
        low_ref[...] = to_low(wide_ref[...])
    block = q_ref.shape[0]
    count = k_ref.shape[0]
    c = HD ** -0.5 * log2e
    def body(at, size):
        near = pl.ds(at, size)
        lane = lax.broadcasted_iota(jnp.int32, (block, PAIR), 1)
        def pair(p, logs):
            cols = pl.ds(pl.multiple_of(p * PAIR, PAIR), PAIR)
            q, k, v = q_ref[:, cols], k_ref[near, cols], v_ref[near, cols]
            hotq, hotk = hotq_ref[...], hotk_ref[near, :]
            fq, fk = first_half(block), first_half(size)
            outs = []
            for h in range(2):
                qh = jnp.where(fq, q, hotq) if h == 0 else jnp.where(fq, hotq, q)
                kh = jnp.where(fk, k, hotk) if h == 0 else jnp.where(fk, hotk, k)
                s = dot(qh, kh, NT)
                top = jnp.max(s, axis=1, keepdims=True) * c
                e = jnp.exp2(s * c - top)
                total = jnp.sum(e, axis=1, keepdims=True)
                o = dot(e.astype(jnp.bfloat16), v)
                outs.append(o * (1.0 / total))
                logs = jnp.where(lane == 2 * p + h, top + jnp.log2(total), logs)
            out_ref[:, cols] = jnp.where(fq, outs[0], outs[1]).astype(jnp.bfloat16)
            return logs
        log_ref[...] = lax.fori_loop(0, pairs, pair, jnp.zeros((block, PAIR), jnp.float32), unroll=unroll)
    windows(span_ref, block, chunk, count, body)

def attend(span, query, key, value, hotq, hotk, casts, block, chunk, unroll):
    count, width = query.shape
    whole = lambda w: pl.BlockSpec((count, w), lambda i, *_: (0, 0))
    part = lambda w: pl.BlockSpec((block, w), lambda i, *_: (i, 0))
    steps = count // block
    slices = [pl.BlockSpec((x.shape[0] // steps, x.shape[1]), lambda i, *_: (i, 0)) for x in casts]
    return pl.pallas_call(
        functools.partial(forward_kernel, width // PAIR, chunk, unroll),
        grid_spec=pltpu.PrefetchScalarGridSpec(
            num_scalar_prefetch=1, grid=(count // block,),
            in_specs=[part(width), whole(width), whole(width), part(PAIR), whole(PAIR)] + slices,
            out_specs=[part(width), part(PAIR)] + slices,
        ),
        out_shape=[jax.ShapeDtypeStruct((count, width), jnp.bfloat16), jax.ShapeDtypeStruct((count, PAIR), jnp.float32)]
        + [jax.ShapeDtypeStruct(x.shape, jnp.bfloat16) for x in casts],
        cost_estimate=small_cost,
        compiler_params=pltpu.CompilerParams(vmem_limit_bytes=62 << 20),
    )(span, query, key, value, hotq, hotk, *casts)

def backward_kernel(
    pairs, chunk, unroll, piece, span_ref, q_ref, k_ref, v_ref, g_ref, hotq_ref, hotk_ref, log_ref, *refs
):
    dq_ref, dk_ref, dv_ref, sums_ref, dk_sum, dv_sum = refs[-6:]
    block = q_ref.shape[0]
    count = k_ref.shape[0]
    c = HD ** -0.5 * log2e
    @pl.when(pl.program_id(0) == 0)
    def _():
        dk_sum[...] = jnp.zeros_like(dk_sum)
        dv_sum[...] = jnp.zeros_like(dv_sum)
        sums_ref[...] = jnp.zeros_like(sums_ref)
    def body(at, size):
        near = pl.ds(at, size)
        lane = lax.broadcasted_iota(jnp.int32, (block, PAIR), 1)
        def pair(p, _):
            cols = pl.ds(pl.multiple_of(p * PAIR, PAIR), PAIR)
            q, k, v, g = q_ref[:, cols], k_ref[near, cols], v_ref[near, cols], g_ref[:, cols]
            hotq, hotk, logs = hotq_ref[...], hotk_ref[near, :], log_ref[...]
            fq, fk = first_half(block), first_half(size)
            zero = jnp.zeros_like(g)
            dqs, dks, dvs = [], [], []
            for h in range(2):
                qh = jnp.where(fq, q, hotq) if h == 0 else jnp.where(fq, hotq, q)
                kh = jnp.where(fk, k, hotk) if h == 0 else jnp.where(fk, hotk, k)
                gh = jnp.where(fq, g, zero) if h == 0 else jnp.where(fq, zero, g)
                s = dot(qh, kh, NT)
                log = jnp.sum(jnp.where(lane == 2 * (p + piece * pairs) + h, logs, 0.0), axis=1, keepdims=True)
                e = jnp.exp2(s * c - log)
                de = dot(gh, v, NT)
                inner = jnp.sum(de * e, axis=1, keepdims=True)
                ds = (e * (de - inner)).astype(jnp.bfloat16)
                dqs.append(dot(ds, k))
                dks.append(dot(ds, q, TN))
                dvs.append(dot(e.astype(jnp.bfloat16), g, TN))
            dq_ref[:, cols] = (jnp.where(fq, dqs[0], dqs[1]) * HD ** -0.5).astype(jnp.bfloat16)
            dk_sum[near, cols] += jnp.where(fk, dks[0], dks[1])
            dv_sum[near, cols] += jnp.where(fk, dvs[0], dvs[1])
            return 0
        lax.fori_loop(0, pairs, pair, 0, unroll=unroll)
    windows(span_ref, block, chunk, count, body)
    rounded = dq_ref[...].astype(jnp.float32)
    sums_ref[0] += jnp.sum(rounded.reshape(-1, 8, rounded.shape[1]), axis=0)
    @pl.when(pl.program_id(0) == pl.num_programs(0) - 1)
    def _():
        sums_ref[1] = jnp.sum(dv_sum[...].reshape(-1, 8, dv_sum.shape[1]), axis=0)
        dk_ref[...] = (dk_sum[...] * HD ** -0.5).astype(jnp.bfloat16)
        dv_ref[...] = dv_sum[...].astype(jnp.bfloat16)

def attend_back(
    span, query, key, value, grad, hotq, hotk, logs, block, chunk, unroll, piece, pieces, after
):
    count = query.shape[0]
    width = query.shape[1] // pieces
    whole = lambda w, j=0: pl.BlockSpec((count, w), lambda i, *_: (0, j))
    part = lambda w, j=0: pl.BlockSpec((block, w), lambda i, *_: (i, j))
    shape = jax.ShapeDtypeStruct
    return pl.pallas_call(
        functools.partial(backward_kernel, width // PAIR, chunk, unroll, piece),
        grid_spec=pltpu.PrefetchScalarGridSpec(
            num_scalar_prefetch=1,
            grid=(count // block,),
            in_specs=[
                part(width, piece),
                whole(width, piece),
                whole(width, piece),
                part(width, piece),
                part(PAIR),
                whole(PAIR),
                part(PAIR),
            ]
            + [pl.BlockSpec(memory_space=pl.ANY)] * len(after),
            out_specs=[
                part(width),
                whole(width),
                whole(width),
                pl.BlockSpec((2, 8, width), lambda i, *_: (0, 0, 0)),
            ],
            scratch_shapes=[pltpu.VMEM((count, width), jnp.float32)] * 2,
        ),
        out_shape=[shape((count, width), jnp.bfloat16)] * 3 + [shape((2, 8, width), jnp.float32)],
        cost_estimate=small_cost,
        compiler_params=pltpu.CompilerParams(vmem_limit_bytes=62 << 20),
    )(span, query, key, value, grad, hotq, hotk, logs, *after)


def attention_plan(lengths_row, segment, count, block, chunk):
    kinds = lengths_row.shape[0]
    bounds = jnp.cumsum(lengths_row)
    starts = bounds - lengths_row
    first = segment[::block]
    last = segment[block - 1 :: block]
    low = starts[first] // chunk
    high = (bounds[last] + chunk - 1) // chunk
    span = jnp.stack([low, high - low]).astype(jnp.int32)
    lane = jnp.arange(PAIR, dtype=jnp.int32)[None, :] % HD
    same = lane == segment[:, None]
    hotq = jnp.where((lane < kinds) & ~same, 1e30, 0.0).astype(jnp.bfloat16)
    hotk = jnp.where(same, -1.0, 0.0).astype(jnp.bfloat16)
    return span, hotq, hotk


def rows_of(values):
    return pl.BlockSpec((values.shape[0], values.shape[1]), lambda i, *_: (0, 0))


def gelu_and_slope(values):
    size = jnp.abs(values) * 0.7071067811865476
    near = 1.0 / (1.0 + 0.3275911 * size)
    bell = jnp.exp2(values * values * (-0.5 * log2e))
    poly = near * (
        0.254829592
        + near * (-0.284496736 + near * (1.421413741 + near * (-1.453152027 + near * 1.061405429)))
    )
    tail = 0.5 * poly * bell
    share = jnp.where(values >= 0, 1.0 - tail, tail)
    return values * share, share + values * bell * 0.3989422804014327


def normalize(values):
    center = values - jnp.mean(values, axis=-1, keepdims=True)
    scale = lax.rsqrt(jnp.mean(center * center, axis=-1, keepdims=True) + norm_eps)
    return center * scale, scale


def normalize_back(grad, normed, scale, gain):
    moved = grad * gain
    inner = (
        moved
        - jnp.mean(moved, axis=-1, keepdims=True)
        - normed * jnp.mean(moved * normed, axis=-1, keepdims=True)
    )
    return inner * scale


def feed_forward_kernel(
    parts,
    attended_ref,
    frames_ref,
    out_ref,
    up_ref,
    down_ref,
    final_ref,
    *refs,
):
    vectors, up_bias_ref, final_bias_ref = refs[:6], refs[6], refs[7]
    (
        hidden_low_ref,
        normed_one_ref,
        active_ref,
        slope_ref,
        normed_two_ref,
        output_low_ref,
        scales_ref,
        unit_ref,
        unit_scale_ref,
    ) = refs[8:]
    vector = lambda row: vectors[row][...].reshape(1, -1)
    resid = frames_ref[...] + dot(attended_ref[...], out_ref[...]) + vector(0)
    normed, scale_one = normalize(resid)
    normed_one_ref[...] = normed
    hidden = normed * vector(1) + vector(2)
    hidden_low = to_low(hidden)
    hidden_low_ref[...] = hidden_low
    second = hidden + vector(3)
    chunk = up_ref.shape[1] // parts
    for part in range(parts):
        at = pl.ds(part * chunk, chunk)
        upper = dot(hidden_low, up_ref[:, at]) + up_bias_ref[at].reshape(1, -1)
        active, slope = gelu_and_slope(upper)
        active = to_low(active)
        active_ref[:, at] = active
        slope_ref[:, at] = to_low(slope)
        second = second + dot(active, down_ref[at, :])
    normed, scale_two = normalize(second)
    normed_two_ref[...] = normed
    output_low = to_low(normed * vector(4) + vector(5))
    output_low_ref[...] = output_low
    final = dot(output_low, final_ref[...]) + final_bias_ref[...].reshape(1, -1)
    turned = final.T
    unit_scale = lax.rsqrt(jnp.sum(turned * turned, axis=0, keepdims=True) + cosine_eps)
    unit_ref[...] = turned * unit_scale
    unit_scale_ref[...] = jnp.broadcast_to(unit_scale, unit_scale_ref.shape)
    lane = lax.broadcasted_iota(jnp.int32, scales_ref.shape, 1)
    scales_ref[...] = jnp.where(lane == 0, scale_one, scale_two)


def feed_forward(attended, frames, out, up, down, final, vectors, block):
    count, model = frames.shape
    inner, width = up.shape[1], final.shape[1]
    part = lambda columns: pl.BlockSpec((block, columns), lambda i: (i, 0))
    turned = lambda rows: pl.BlockSpec((rows, block), lambda i: (0, i))
    shape = jax.ShapeDtypeStruct
    low, full = jnp.bfloat16, jnp.float32
    operands = (attended, frames, out, up, down, final)
    return pl.pallas_call(
        functools.partial(feed_forward_kernel, max(inner // model, 1)),
        grid=(count // block,),
        in_specs=[part(model), part(model)]
        + [rows_of(x) for x in operands[2:]]
        + [vector_spec(x) for x in vectors],
        out_specs=[part(model), part(model), part(inner), part(inner), part(model), part(model), part(PAIR)]
        + [turned(width), turned(8)],
        out_shape=[
            shape((count, model), low),
            shape((count, model), full),
            shape((count, inner), low),
            shape((count, inner), low),
            shape((count, model), full),
            shape((count, model), low),
            shape((count, PAIR), full),
            shape((width, count), full),
            shape((8, count), full),
        ],
        cost_estimate=small_cost,
        compiler_params=pltpu.CompilerParams(vmem_limit_bytes=62 << 20),
    )(*operands, *vectors)


def feed_forward_back_kernel(
    parts,
    d_final_ref,
    slope_ref,
    normed_one_ref,
    normed_two_ref,
    scales_ref,
    final_ref,
    up_ref,
    down_ref,
    out_ref,
    gain_one_ref,
    gain_two_ref,
    down_low_ref,
    upper_low_ref,
    resid_ref,
    branch_low_ref,
    attended_low_ref,
    sums_ref,
    up_sums_ref,
):
    @pl.when(pl.program_id(0) == 0)
    def _():
        sums_ref[...] = jnp.zeros_like(sums_ref)
        up_sums_ref[...] = jnp.zeros_like(up_sums_ref)

    def add(row, values):
        sums_ref[row] += jnp.sum(values.reshape(-1, 8, values.shape[1]), axis=0)

    grad = dot(d_final_ref[...], final_ref[...], NT)
    normed = normed_two_ref[...]
    gain = gain_two_ref[...].reshape(1, -1)
    hidden = normalize_back(grad, normed, scales_ref[:, 1:2], gain)
    down_low = to_low(hidden)
    down_low_ref[...] = down_low
    add(0, grad * normed)
    add(1, grad)
    add(2, down_low.astype(jnp.float32))
    chunk = up_ref.shape[1] // parts
    for part in range(parts):
        at = pl.ds(part * chunk, chunk)
        upper = dot(down_low, down_ref[at, :], NT) * slope_ref[:, at].astype(jnp.float32)
        upper_low = to_low(upper)
        upper_low_ref[:, at] = upper_low
        up_sums_ref[:, at] += jnp.sum(upper.reshape(-1, 8, chunk), axis=0)
        hidden = hidden + dot(upper_low, up_ref[:, at], NT)
    normed = normed_one_ref[...]
    gain = gain_one_ref[...].reshape(1, -1)
    resid = normalize_back(hidden, normed, scales_ref[:, 0:1], gain)
    resid_ref[...] = resid
    branch_low = to_low(resid)
    branch_low_ref[...] = branch_low
    attended_low_ref[...] = to_low(dot(branch_low, out_ref[...], NT))
    add(3, hidden * normed)
    add(4, hidden)
    add(5, branch_low.astype(jnp.float32))


def feed_forward_back(d_final, slope, normed_one, normed_two, scales, final, up, down, out, gains, block):
    count, model = normed_one.shape
    inner = up.shape[1]
    part = lambda columns: pl.BlockSpec((block, columns), lambda i: (i, 0))
    shape = jax.ShapeDtypeStruct
    low, full = jnp.bfloat16, jnp.float32
    return pl.pallas_call(
        functools.partial(feed_forward_back_kernel, max(inner // model, 1)),
        grid=(count // block,),
        in_specs=[part(d_final.shape[1]), part(inner), part(model), part(model), part(PAIR)]
        + [rows_of(x) for x in (final, up, down, out)]
        + [vector_spec(x) for x in gains],
        out_specs=[part(model), part(inner), part(model), part(model), part(model)]
        + [
            pl.BlockSpec((6, 8, model), lambda i: (0, 0, 0)),
            pl.BlockSpec((8, inner), lambda i: (0, 0)),
        ],
        out_shape=[
            shape((count, model), low),
            shape((count, inner), low),
            shape((count, model), full),
            shape((count, model), low),
            shape((count, model), low),
            shape((6, 8, model), full),
            shape((8, inner), full),
        ],
        cost_estimate=small_cost,
        compiler_params=pltpu.CompilerParams(vmem_limit_bytes=62 << 20),
    )(d_final, slope, normed_one, normed_two, scales, final, up, down, out, *gains)


def candidate_kernel(
    slots, owners, keep, index_ref, rows_ref, unit_ref, scale_ref, positive_ref, masked_ref,
    loss_ref, final_low_ref, positive_part_ref, rows_grad_ref,
    packed, mass, pull, total, unit_low, weighted,
):
    step = pl.program_id(0)
    frames = unit_ref.shape[1]
    own = rows_ref.shape[0]
    lanes = 128
    words = lax.broadcasted_iota(jnp.int32, (128, lanes), 0)

    def fill(at_mass):
        def count(tile, _):
            at = pl.ds(pl.multiple_of(tile * lanes, lanes), lanes)
            acc = jnp.zeros((128, lanes), jnp.int32)
            for slot in range(slots):
                index = index_ref[0, pl.ds(slot, 1), at]
                low = jnp.bitwise_and(index, 127)
                unit = jnp.where(index >= 0, jnp.left_shift(1, 4 * jnp.right_shift(index, 7)), 0)
                acc = acc + jnp.where(words == low, unit, 0)
            packed[:, at] = acc
            return 0

        lax.fori_loop(0, frames // lanes, count, 0)

        def part(nibble, _):
            at = pl.ds(pl.multiple_of(nibble * 128, 128), 128)
            cosine = dot(rows_ref[at, :], unit_low[...])
            times = jnp.bitwise_and(lax.shift_right_logical(packed[...], 4 * nibble), 15)
            value = times.astype(jnp.float32) * jnp.exp2(cosine)
            total[...] += jnp.sum(value.reshape(16, 8, frames), axis=0)
            mass[pl.ds(pl.multiple_of(at_mass + nibble * 128, 128), 128), :] = to_low(value)
            return 0

        lax.fori_loop(0, own // 128, part, 0, unroll=2)

    @pl.when(step == 0)
    def _():
        unit_low[...] = to_low(unit_ref[...])
        total[...] = jnp.zeros_like(total)
        pull[...] = jnp.zeros_like(pull)

    @pl.when(step < owners)
    def _():
        at_mass = step * own if keep else 0
        fill(at_mass)
        pull[...] += dot(rows_ref[...], mass[pl.ds(pl.multiple_of(at_mass, own), own), :], TN)

    @pl.when(step == owners - 1)
    def _():
        score_scale = log2e / similarity_softening_factor
        unit, positive, masked = unit_ref[...], positive_ref[...], masked_ref[...]
        mass_sum = jnp.sum(total[...], axis=0, keepdims=True)
        score = jnp.sum(unit * positive, axis=0, keepdims=True) * (1.0 / similarity_softening_factor)
        whole = jnp.exp(score) + mass_sum
        loss_ref[...] = jnp.broadcast_to(masked * (jnp.log(whole) - score), loss_ref.shape)
        weight = masked / whole * (1.0 / similarity_softening_factor)
        d_score = -weight * mass_sum
        d_unit = d_score * positive + weight * (1.0 / score_scale) * pull[...]
        inner = jnp.sum(d_unit * unit, axis=0, keepdims=True)
        final_low_ref[...] = to_low((scale_ref[0:1, :] * (d_unit - unit * inner)).T)
        positive_part_ref[...] = (d_score * unit).T
        weighted[...] = to_low((weight * unit).T)

    @pl.when(step >= owners)
    def _():
        at_mass = (step - owners) * own if keep else 0
        if not keep:
            fill(at_mass)
        rows_grad_ref[...] = to_low(dot(mass[pl.ds(pl.multiple_of(at_mass, own), own), :], weighted[...]))


def candidates(index, rows, unit, scale, positive, masked):
    owners, slots, frames = index.shape
    width = rows.shape[1]
    own = rows.shape[0] // owners
    keep = rows.shape[0] * frames * 2 <= 16 << 20
    again = (lambda i: jnp.minimum(i, owners - 1)) if keep else (lambda i: lax.rem(i, owners))
    shape = jax.ShapeDtypeStruct
    return pl.pallas_call(
        functools.partial(candidate_kernel, slots, owners, keep),
        grid=(2 * owners,),
        in_specs=[
            pl.BlockSpec((1, slots, frames), lambda i: (again(i), 0, 0)),
            pl.BlockSpec((own, width), lambda i: (again(i), 0)),
            rows_of(unit),
            rows_of(scale),
            rows_of(positive),
            rows_of(masked),
        ],
        out_specs=[
            pl.BlockSpec((8, frames), lambda i: (0, 0)),
            pl.BlockSpec((frames, width), lambda i: (0, 0)),
            pl.BlockSpec((frames, width), lambda i: (0, 0)),
            pl.BlockSpec((own, width), lambda i: (jnp.maximum(i - owners, 0), 0)),
        ],
        out_shape=[
            shape((8, frames), jnp.float32),
            shape((frames, width), jnp.bfloat16),
            shape((frames, width), jnp.float32),
            shape((rows.shape[0], width), jnp.bfloat16),
        ],
        scratch_shapes=[
            pltpu.VMEM((128, frames), jnp.int32),
            pltpu.VMEM((rows.shape[0] if keep else own, frames), jnp.bfloat16),
            pltpu.VMEM((width, frames), jnp.float32),
            pltpu.VMEM((8, frames), jnp.float32),
            pltpu.VMEM((width, frames), jnp.bfloat16),
            pltpu.VMEM((frames, width), jnp.bfloat16),
        ],
        cost_estimate=small_cost,
        compiler_params=pltpu.CompilerParams(vmem_limit_bytes=62 << 20),
    )(index, rows, unit, scale, positive, masked)


def down_grad_kernel(active_ref, grad_ref, *refs):
    out_ref, turned = refs[-2:]

    @pl.when(pl.program_id(0) == 0)
    def _():
        turned[...] = grad_ref[...].T

    out_ref[...] = to_low(dot(turned[...], active_ref[...])).reshape(out_ref.shape)


def down_grad(active, grad, members, groups, after):
    count, inner = active.shape
    model = grad.shape[1]
    share = inner // members
    block = (1, groups, model // groups, share)
    return pl.pallas_call(
        down_grad_kernel,
        grid=(members,),
        in_specs=[
            pl.BlockSpec((count, share), lambda i: (0, i)),
            pl.BlockSpec((count, model), lambda i: (0, 0)),
        ]
        + [pl.BlockSpec(memory_space=pl.ANY)] * len(after),
        out_specs=pl.BlockSpec(block, lambda i: (i, 0, 0, 0)),
        out_shape=jax.ShapeDtypeStruct((members, groups, model // groups, share), jnp.bfloat16),
        scratch_shapes=[pltpu.VMEM((model, count), jnp.bfloat16)],
        cost_estimate=small_cost,
        compiler_params=pltpu.CompilerParams(vmem_limit_bytes=62 << 20),
    )(active, grad, *after)


def up_grad_kernel(
    groups, core_ref, hidden_ref, upper_ref, attended_ref, branch_ref, output_ref, final_ref, *refs
):
    kept_ref, sent_ref, turned, attended_turned, held = refs[-5:]
    group = pl.program_id(0)
    core = core_ref[0]
    lines, share = kept_ref.shape[1], kept_ref.shape[2]

    @pl.when(group == 0)
    def _():
        turned[...] = hidden_ref[...].T
        attended_turned[...] = attended_ref[...].T

    wide = upper_ref.shape[1]
    side = final_ref.shape[1]
    held[:, :, :, :wide] = to_low(dot(turned[...], upper_ref[...])).reshape(lines, 2, share, wide)

    @pl.when(group < groups - 1)
    def _():
        value = dot(attended_turned[...], branch_ref[...])
        held[:, :, :, wide:] = to_low(value).reshape(lines, 2, share, side)

    @pl.when(group == groups - 1)
    def _():
        value = dot(output_ref[...], final_ref[...], TN)
        held[:, :, :, wide:] = to_low(value).reshape(lines, 2, share, side)

    kept_ref[0] = held[:, core]
    sent_ref[0] = held[:, 1 - core]


def up_grad(core, hidden, upper, attended, branch, output, final, members, groups, after):
    count, model = hidden.shape
    wide, side = upper.shape[1] // groups, final.shape[1]
    lines, share = members // 2, model // members
    whole = lambda columns: pl.BlockSpec((count, columns), lambda g, core: (0, 0))
    out = pl.BlockSpec((1, lines, share, wide + side), lambda g, core: (g, 0, 0, 0))
    shape = jax.ShapeDtypeStruct((groups, lines, share, wide + side), jnp.bfloat16)
    last = model // side - 1
    return pl.pallas_call(
        functools.partial(up_grad_kernel, groups),
        grid_spec=pltpu.PrefetchScalarGridSpec(
            num_scalar_prefetch=1,
            grid=(groups,),
            in_specs=[
                whole(model),
                pl.BlockSpec((count, wide), lambda g, core: (0, g)),
                whole(model),
                pl.BlockSpec((count, side), lambda g, core: (0, jnp.minimum(g, last))),
                whole(model),
                whole(side),
            ]
            + [pl.BlockSpec(memory_space=pl.ANY)] * len(after),
            out_specs=[out, out],
            scratch_shapes=[
                pltpu.VMEM((model, count), jnp.bfloat16),
                pltpu.VMEM((model, count), jnp.bfloat16),
                pltpu.VMEM((lines, 2, share, wide + side), jnp.bfloat16),
            ],
        ),
        out_shape=[shape, shape],
        cost_estimate=small_cost,
        compiler_params=pltpu.CompilerParams(vmem_limit_bytes=62 << 20),
    )(core, hidden, upper, attended, branch, output, final, *after)


def projection_grad_kernel(grads, core_ref, frames_ref, *refs):
    kept_ref, sent_ref, held = refs[-3:]
    core = core_ref[0]
    turned = frames_ref[...].T
    each = kept_ref.shape[3] // PAIR
    tile = 0
    for number, ref in enumerate(refs[:grads]):
        if len(ref.shape) == 2:
            held[...] = to_low(dot(turned, ref[...])).reshape(held.shape)
        else:
            held[...] = ref[...]
        for column in range(held.shape[3] // PAIR):
            group, lanes = tile // each, pl.ds(tile % each * PAIR, PAIR)
            at = pl.ds(column * PAIR, PAIR)
            kept_ref[group, :, :, lanes] = held[:, core, :, at]
            sent_ref[group, :, :, lanes] = held[:, 1 - core, :, at]
            tile += 1


def projection_grad(core, frames, grads, extra, members, groups, after):
    count, model = frames.shape
    lines, share = members // 2, model // members
    pieces = [*grads, *extra]
    width = grads[0].shape[1]
    shape = jax.ShapeDtypeStruct((groups, lines, share, len(pieces) * width // groups), jnp.bfloat16)
    vmem = pl.BlockSpec(memory_space=pltpu.VMEM)
    return pl.pallas_call(
        functools.partial(projection_grad_kernel, len(pieces)),
        in_specs=[pl.BlockSpec(memory_space=pltpu.SMEM)]
        + [vmem] * (1 + len(pieces))
        + [pl.BlockSpec(memory_space=pl.ANY)] * len(after),
        out_specs=[vmem, vmem],
        out_shape=[shape, shape],
        scratch_shapes=[pltpu.VMEM((lines, 2, share, width), jnp.bfloat16)],
        cost_estimate=small_cost,
        compiler_params=pltpu.CompilerParams(vmem_limit_bytes=62 << 20),
    )(core, frames, *pieces, *after)


def slot_rows(distractors, members):
    count, slots = distractors.shape
    turns = -(-slots // members)
    padded = jnp.pad(distractors, ((0, 0), (0, turns * members - slots)), constant_values=-1)
    padded = padded.T.reshape(turns, members, count)
    period = members // math.gcd(slots, members)
    frame = jnp.arange(count, dtype=jnp.int32) % period
    placed = padded
    for phase in range(1, period):
        turned = jnp.roll(padded, phase * slots % members, axis=1)
        placed = jnp.where(frame == phase, turned, placed)
    return placed.transpose(1, 0, 2)


def target_kernel(came_ref, part_ref, unit_ref, scale_ref, low_ref, matrix_ref, *refs):
    grad_ref, matrix_grad_ref, sums_ref = refs[-3:]
    grad_unit = part_ref[...] + came_ref[...].astype(jnp.float32)
    unit = unit_ref[...]
    inner = jnp.sum(grad_unit * unit, axis=-1, keepdims=True)
    low = to_low(scale_ref[:, 0:1] * (grad_unit - unit * inner))
    grad_ref[...] = dot(low, to_low(matrix_ref[...]), NT)
    matrix_grad_ref[...] = dot(to_low(low_ref[...]), low, TN)
    sums_ref[...] = jnp.sum(low.astype(jnp.float32).reshape(-1, 8, low.shape[1]), axis=0)


def target_back(came, part, unit, scale, low, matrix, after):
    count, width = part.shape
    vmem = pl.BlockSpec(memory_space=pltpu.VMEM)
    shape = jax.ShapeDtypeStruct
    return pl.pallas_call(
        target_kernel,
        in_specs=[vmem] * 6 + [pl.BlockSpec(memory_space=pl.ANY)] * len(after),
        out_specs=[vmem] * 3,
        out_shape=[
            shape((count, width), jnp.float32),
            shape((width, width), jnp.float32),
            shape((8, width), jnp.float32),
        ],
        cost_estimate=small_cost,
        compiler_params=pltpu.CompilerParams(vmem_limit_bytes=62 << 20),
    )(came, part, unit, scale, low, matrix, *after)


def inputs_kernel(parts, resid_ref, *refs):
    out_ref, low_ref = refs[-2:]

    @pl.when(pl.program_id(0) == 0)
    def _():
        for matrix in range(3):
            low_ref[matrix] = to_low(refs[3 * parts + matrix][...])

    total = resid_ref[...]
    for matrix in range(3):
        low = 0
        for part in range(parts):
            grad_ref = refs[matrix * parts + part]
            high = low + grad_ref.shape[1]
            total = total + dot(grad_ref[...], low_ref[matrix, :, low:high], NT)
            low = high
    out_ref[...] = total


def inputs_back(resid, grads, matrices, block, after):
    count, model = resid.shape
    part = lambda x: pl.BlockSpec((block, x.shape[1]), lambda i: (i, 0))
    flat = [g for parts in grads for g in parts]
    return pl.pallas_call(
        functools.partial(inputs_kernel, len(grads[0])),
        grid=(count // block,),
        in_specs=[part(resid)]
        + [part(g) for g in flat]
        + [rows_of(m) for m in matrices]
        + [pl.BlockSpec(memory_space=pl.ANY)] * len(after),
        out_specs=part(resid),
        out_shape=jax.ShapeDtypeStruct(resid.shape, jnp.float32),
        scratch_shapes=[pltpu.VMEM((3, model, model), jnp.bfloat16)],
        cost_estimate=small_cost,
        compiler_params=pltpu.CompilerParams(vmem_limit_bytes=62 << 20),
    )(resid, *flat, *matrices, *after)


def target_prepare_kernel(targets_ref, matrix_ref, bias_ref, rows_ref, unit_ref, turned_ref, scale_ref):
    low = to_low(dot(to_low(targets_ref[...]), to_low(matrix_ref[...])) + bias_ref[...].reshape(1, -1))
    positive = low.astype(jnp.float32)
    scale = lax.rsqrt(jnp.sum(positive * positive, axis=-1, keepdims=True) + cosine_eps)
    unit = positive * scale
    rows_ref[...] = to_low(unit * (log2e / similarity_softening_factor))
    unit_ref[...] = unit
    turned_ref[...] = unit.T
    scale_ref[...] = jnp.broadcast_to(scale, scale_ref.shape)


def target_prepare(targets, matrix, bias):
    count, width = targets.shape
    vmem = pl.BlockSpec(memory_space=pltpu.VMEM)
    shape = jax.ShapeDtypeStruct
    return pl.pallas_call(
        target_prepare_kernel,
        in_specs=[vmem] * 3,
        out_specs=[vmem] * 4,
        out_shape=[
            shape((count, width), jnp.bfloat16),
            shape((count, width), jnp.float32),
            shape((width, count), jnp.float32),
            shape((count, PAIR), jnp.float32),
        ],
        cost_estimate=small_cost,
        compiler_params=pltpu.CompilerParams(vmem_limit_bytes=62 << 20),
    )(targets, matrix, bias)


def project_kernel(frames_ref, wq_ref, wk_ref, wv_ref, bq_ref, bv_ref, *refs):
    low_ref, q_ref, k_ref, v_ref, mq, mk, mv = refs[-7:]

    @pl.when(pl.program_id(0) == 0)
    def _():
        mq[...] = to_low(wq_ref[...])
        mk[...] = to_low(wk_ref[...])
        mv[...] = to_low(wv_ref[...])

    low = to_low(frames_ref[...])
    low_ref[...] = low
    q_ref[...] = to_low(dot(low, mq[...]) + bq_ref[...].reshape(1, -1))
    k_ref[...] = to_low(dot(low, mk[...]))
    v_ref[...] = to_low(dot(low, mv[...]) + bv_ref[...].reshape(1, -1))


def vector_spec(values):
    return pl.BlockSpec(values.shape, lambda i, *_: (0,))


def project(frames, w_query, w_key, w_value, b_query, b_value, block, after):
    count, model = frames.shape
    part = pl.BlockSpec((block, model), lambda i: (i, 0))
    return pl.pallas_call(
        project_kernel,
        grid=(count // block,),
        in_specs=[part]
        + [rows_of(w) for w in (w_query, w_key, w_value)]
        + [vector_spec(b) for b in (b_query, b_value)]
        + [pl.BlockSpec(memory_space=pl.ANY)] * len(after),
        out_specs=[part] * 4,
        out_shape=[jax.ShapeDtypeStruct((count, model), jnp.bfloat16)] * 4,
        scratch_shapes=[pltpu.VMEM((model, model), jnp.bfloat16)] * 3,
        cost_estimate=small_cost,
        compiler_params=pltpu.CompilerParams(vmem_limit_bytes=62 << 20),
    )(frames, w_query, w_key, w_value, b_query, b_value, *after)


def exchange(sent):
    members = lax.axis_size("tm")
    return lax.ppermute(sent, "tm", [(i, i ^ 1) for i in range(members)])


def split_kernel(counts, pieces, choice_ref, *refs):
    out_refs = refs[-pieces:]
    number, low, lanes = 0, 0, 0
    for count in counts:
        total = refs[number][0].astype(jnp.float32)
        for term in range(1, count):
            total = total + refs[number + term][0].astype(jnp.float32)
        total = to_low(total)
        high = lanes + total.shape[-1]
        for piece in range(pieces):

            @pl.when(pl.program_id(0) == piece)
            def _(piece=piece, total=total, low=low, lanes=lanes, high=high):
                if total.ndim == 3:
                    out_refs[piece][low : low + total.shape[0]] = total
                else:
                    out_refs[piece][:, lanes:high] = total

        number, low, lanes = number + count, low + total.shape[0], high


def split_sum(choice, sums, pieces, after):
    terms = [term for group in sums for term in group]
    first = [group[0].shape[1:] for group in sums]
    if len(first[0]) == 3:
        rest = (sum(shape[0] for shape in first), *first[0][1:])
    else:
        rest = (first[0][0], sum(shape[1] for shape in first))

    def source(term):
        zeros = (0,) * (term.ndim - 1)
        return pl.BlockSpec((1, *term.shape[1:]), lambda i, choice: (choice[0] ^ i, *zeros))

    return pl.pallas_call(
        functools.partial(split_kernel, [len(group) for group in sums], pieces),
        grid_spec=pltpu.PrefetchScalarGridSpec(
            num_scalar_prefetch=1,
            grid=(pieces,),
            in_specs=[source(term) for term in terms]
            + [pl.BlockSpec(memory_space=pl.ANY)] * len(after),
            out_specs=[pl.BlockSpec(rest, lambda i, choice: (0,) * len(rest))] * pieces,
        ),
        out_shape=[jax.ShapeDtypeStruct(rest, jnp.bfloat16)] * pieces,
        cost_estimate=small_cost,
        compiler_params=pltpu.CompilerParams(vmem_limit_bytes=62 << 20),
    )(choice, *terms, *after)


def swap(pieces, axis="grp", stride=1):
    size = lax.axis_size(axis)
    return [pieces[0]] + [
        lax.ppermute(piece, axis, [(i, i ^ (k * stride)) for i in range(size)])
        for k, piece in enumerate(pieces)
        if k
    ]


def line_kernel(terms, *refs):
    total = refs[0][...].astype(jnp.float32)
    for term in range(1, terms):
        total = total + refs[term][...].astype(jnp.float32)
    refs[-1][...] = to_low(total)


def line_sum(terms, after):
    lines, rest = terms[0].shape[0], terms[0].shape[1:]
    block = pl.BlockSpec((1, *rest), lambda i: (i, *(0,) * len(rest)))
    return pl.pallas_call(
        functools.partial(line_kernel, len(terms)),
        grid=(lines,),
        in_specs=[block] * len(terms) + [pl.BlockSpec(memory_space=pl.ANY)] * len(after),
        out_specs=block,
        out_shape=jax.ShapeDtypeStruct(terms[0].shape, jnp.bfloat16),
        cost_estimate=small_cost,
        compiler_params=pltpu.CompilerParams(vmem_limit_bytes=62 << 20),
    )(*terms, *after)


def core_pairs():
    return [[2 * i, 2 * i + 1] for i in range(lax.axis_size("tm") // 2)]


def chip_lines():
    return [list(range(first, lax.axis_size("tm"), 2)) for first in range(2)]


def scatter(value, axis, among=None):
    return lax.psum_scatter(value, axis, scatter_dimension=0, axis_index_groups=among)


def over_lines(value):
    return lax.all_to_all(value, "tm", 0, 0, tiled=True, axis_index_groups=chip_lines())


def share_kernel(start, done_ref, line_ref, out_ref):
    wide = done_ref.shape[2]
    total = line_ref[0].astype(jnp.float32)
    for term in range(1, line_ref.shape[0]):
        total = total + line_ref[term].astype(jnp.float32)
    total = to_low(total)
    for copy in range(out_ref.shape[0]):
        low = 0
        for at in range(start, done_ref.shape[0]):
            out_ref[copy, :, low : low + wide] = done_ref[at]
            low += wide
        out_ref[copy, :, low:] = total


def shares(done, lines, start, groups):
    rows = done.shape[1]
    wide = (done.shape[0] - start) * done.shape[2] + lines.shape[2]
    vmem = pl.BlockSpec(memory_space=pltpu.VMEM)
    return pl.pallas_call(
        functools.partial(share_kernel, start),
        in_specs=[vmem] * 2,
        out_specs=vmem,
        out_shape=jax.ShapeDtypeStruct((groups, rows, wide), jnp.bfloat16),
        cost_estimate=small_cost,
        compiler_params=pltpu.CompilerParams(vmem_limit_bytes=62 << 20),
    )(done, lines)


def place(kernel, arrays, shapes, after, choice=None):
    vmem = pl.BlockSpec(memory_space=pltpu.VMEM)
    first = [] if choice is None else [choice]
    used = len(first) + len(arrays)
    return pl.pallas_call(
        lambda *refs: kernel(*refs[:used], *refs[used + len(after) :]),
        in_specs=[pl.BlockSpec(memory_space=pltpu.SMEM)] * len(first)
        + [vmem] * len(arrays)
        + [pl.BlockSpec(memory_space=pl.ANY)] * len(after),
        out_specs=[vmem] * len(shapes),
        out_shape=[jax.ShapeDtypeStruct(s, jnp.float32) for s in shapes],
        cost_estimate=small_cost,
        compiler_params=pltpu.CompilerParams(vmem_limit_bytes=62 << 20),
    )(*first, *arrays, *after)


def line_total(terms, after):
    vmem = pl.BlockSpec(memory_space=pltpu.VMEM)
    return pl.pallas_call(
        functools.partial(line_kernel, len(terms)),
        in_specs=[vmem] * len(terms) + [pl.BlockSpec(memory_space=pl.ANY)] * len(after),
        out_specs=vmem,
        out_shape=jax.ShapeDtypeStruct(terms[0].shape, jnp.bfloat16),
        cost_estimate=small_cost,
        compiler_params=pltpu.CompilerParams(vmem_limit_bytes=62 << 20),
    )(*terms, *after)


def on_device(
    frames,
    targets,
    lengths,
    span_starts,
    distractors,
    w_query,
    b_query,
    w_key,
    w_value,
    b_value,
    w_out,
    b_out,
    norm_gain,
    norm_bias,
    w_up,
    b_up,
    w_down,
    b_down,
    final_gain,
    final_bias,
    w_final,
    b_final,
    w_target,
    b_target,
):
    count, model = frames.shape
    width = targets.shape[1]
    inner = w_up.shape[1]
    members, groups = lax.axis_size("tm"), lax.axis_size("grp")
    block = min(count, 256)
    share = model // members
    place_in_line = lax.axis_index("tm")
    core = (place_in_line % 2)[None].astype(jnp.int32)
    line = (place_in_line // 2)[None].astype(jnp.int32)
    group = lax.axis_index("grp")[None].astype(jnp.int32)

    own_rows, positive_unit, positive_turned, positive_scale = target_prepare(targets, w_target, b_target)
    rows = lax.all_gather(own_rows, "tm", tiled=True)
    index = slot_rows(distractors, members)

    segment = segment_ids(lengths[0], count)
    masked = span_mask(span_starts, segment, count)
    span, hot_query, hot_key = attention_plan(lengths[0], segment, count, block, block)
    frames_low, query, key, value = project(
        frames, w_query, w_key, w_value, b_query, b_value, block, (own_rows,)
    )
    attended_low, log_total, out_matrix, up_matrix, down_matrix, final_matrix = attend(
        span, query, key, value, hot_query, hot_key, (w_out, w_up, w_down, w_final), block, block, 2
    )
    (
        hidden_low,
        normed_one,
        active_low,
        slope,
        normed_two,
        output_low,
        scales,
        final_unit,
        final_scale,
    ) = feed_forward(
        attended_low,
        frames,
        out_matrix,
        up_matrix,
        down_matrix,
        final_matrix,
        (b_out, norm_gain, norm_bias, b_down, final_gain, final_bias, b_up, b_final),
        block,
    )
    losses, d_final_low, positive_part, d_rows = candidates(
        index, rows, final_unit, final_scale, positive_turned, masked[None]
    )
    came = lax.psum_scatter(d_rows, "tm", scatter_dimension=0, tiled=True)

    d_down_low, d_upper_low, d_resid, d_branch_low, d_attended_low, model_sums, up_sums = feed_forward_back(
        d_final_low,
        slope,
        normed_one,
        normed_two,
        scales,
        final_matrix,
        up_matrix,
        down_matrix,
        out_matrix,
        (norm_gain, final_gain),
        block,
    )
    def attention_back(piece, pieces, after):
        return attend_back(
            span,
            query,
            key,
            value,
            d_attended_low,
            hot_query,
            hot_key,
            log_total,
            block,
            block,
            2,
            piece,
            pieces,
            after,
        )


    def total(values):
        return jnp.sum(values, axis=0)

    def vector_sums(piece_sums, target_sums):
        return (
            jnp.concatenate([total(s[0]) for s in piece_sums]),
            jnp.concatenate([total(s[1]) for s in piece_sums]),
            total(model_sums[5]),
            total(model_sums[3]),
            total(model_sums[4]),
            total(up_sums),
            total(model_sums[2]),
            total(model_sums[0]),
            total(model_sums[1]),
            column_sum(d_final_low),
            total(target_sums),
        )

    if share % 16 or (inner // members) % PAIR or model != (groups - 1) * width:
        back = [attention_back(piece, 3, ()) for piece in range(3)]
        d_query, d_key, d_value, piece_sums = ([part[k] for part in back] for k in range(4))
        target_grad, grad_w_target, target_sums = target_back(
            came, positive_part, positive_unit, positive_scale, targets, w_target, ()
        )
        input_grad = inputs_back(
            d_resid, (d_query, d_key, d_value), (w_query, w_key, w_value), block, ()
        )

        def reduced(grad):
            part = lax.psum_scatter(grad, "tm", scatter_dimension=0, tiled=True)
            return lax.psum(to_low(part), "grp").astype(jnp.float32)

        def projected(parts):
            return reduced(product_left(frames_low, jnp.concatenate(parts, axis=1)))

        small = [reduced(vector) for vector in vector_sums(piece_sums, target_sums)]
        return (
            losses[0],
            input_grad,
            target_grad,
            projected(d_query),
            small[0],
            projected(d_key),
            projected(d_value),
            small[1],
            reduced(product_left(attended_low, d_branch_low)),
            small[2],
            small[3],
            small[4],
            reduced(product_left(hidden_low, d_upper_low)),
            small[5],
            reduced(product_left(active_low, d_down_low)),
            small[6],
            small[7],
            small[8],
            reduced(product_left(output_low, d_final_low)),
            small[9],
            reduced(grad_w_target),
            small[10],
        )

    down_parts = down_grad(active_low, d_down_low, members, groups, ())
    down_part = scatter(down_parts, "tm")
    up_kept, up_sent = up_grad(
        core,
        hidden_low,
        d_upper_low,
        attended_low,
        d_branch_low,
        output_low,
        d_final_low,
        members,
        groups,
        (down_parts,),
    )
    up_came = exchange(up_sent)
    target_grad, grad_w_target, target_sums = target_back(
        came, positive_part, positive_unit, positive_scale, targets, w_target, (up_sent,)
    )
    up_group = split_sum(group, [[up_kept, up_came]], groups, (grad_w_target,))
    up_groups = swap(up_group)

    def projections(pieces, extra, after):
        grads = [back[piece][k] for k in range(3) for piece in pieces]
        return projection_grad(core, frames_low, grads, extra, members, groups, after)

    back = [attention_back(0, 3, (up_group[1],))]
    back.append(attention_back(1, 3, (back[0][0],)))
    early_kept, early_sent = projections((0, 1), [], (back[1][0],))
    early_came = exchange(early_sent)
    up_line = line_sum(up_groups, (early_sent,))
    up_lines = over_lines(up_line)
    early_group = split_sum(
        group,
        [[early_kept, early_came], [down_part.reshape(groups, -1, share, inner // members)]],
        groups,
        (up_line,),
    )
    early_groups = swap(early_group)
    back.append(attention_back(2, 3, (early_group[1],)))
    early_line = line_sum(early_groups, (back[2][0],))
    most_shares = shares(early_line, up_lines, members // 2, groups)
    most = lax.all_to_all(most_shares, "grp", 0, 0, tiled=True)
    d_query, d_key, d_value, piece_sums = ([part[k] for part in back] for k in range(4))
    summed = vector_sums(piece_sums, target_sums)
    lines_of = []
    for vector in summed:
        part = vector.reshape(members, -1)
        lanes = -(-part.shape[1] // PAIR) * PAIR
        part = jnp.pad(part, ((0, 0), (0, lanes - part.shape[1])))
        lines_of.append(part.reshape(members, -1, PAIR))
    counts = [part.shape[1] for part in lines_of]
    joined = jnp.concatenate(lines_of, axis=1)
    square = grad_w_target.reshape(members, width // members, width // PAIR, PAIR)
    square = square.transpose(0, 2, 1, 3).reshape(members, -1, PAIR)
    extra = jnp.concatenate(
        [jnp.pad(x, ((0, 0), (0, share - x.shape[1]), (0, 0))) for x in (joined, square)], axis=2
    )
    extra = to_low(extra).reshape(members // 2, 2, share, 2 * PAIR)
    late_kept, late_sent = projections((2,), [extra], (most_shares,))
    late_came = exchange(late_sent)
    late_group = split_sum(group, [[late_kept, late_came]], groups, (most,))
    late_groups = swap(late_group)
    input_grad = inputs_back(
        d_resid, (d_query, d_key, d_value), (w_query, w_key, w_value), block, (late_group[1],)
    )
    own_line = split_sum(line, [[early_line], late_groups], members // 2, (input_grad,))
    own_lines = swap(own_line, "tm", 2)
    up_at = inner // members * (model // groups // share)
    side_at = up_at + inner // groups

    def put_most(most_ref, down_ref, up_ref, out_ref, final_ref):
        rows = model // groups
        for at in range(groups):
            part = lambda low, high: most_ref[at, :, low:high].astype(jnp.float32)
            for top in range(rows // share):
                low = at * rows + top * share
                wide = inner // members
                down_ref[:, low : low + share] = part(top * wide, (top + 1) * wide).T
            wide = inner // groups
            up_ref[:, at * wide : (at + 1) * wide] = part(up_at, side_at)
            if at < groups - 1:
                out_ref[:, at * width : (at + 1) * width] = part(side_at, side_at + width)
            else:
                final_ref[...] = part(side_at, side_at + width)

    grad_down, grad_up, grad_out, grad_final = place(
        put_most,
        [most],
        [(inner // members, model), (share, inner), (share, model), (share, width)],
        (own_line[1],),
    )
    last = swap([line_total(own_lines, (grad_down,))] * groups)
    third = model // 3
    early = [(k, piece * third + at) for k in range(3) for piece in (0, 1) for at in range(0, third, PAIR)]
    late = [(k, 2 * third + at) for k in range(3) for at in range(0, third, PAIR)]
    late += [(3, at) for at in range(0, 2 * PAIR, PAIR)]

    def put_last(choice_ref, *refs):
        outs = refs[groups:]
        for piece in range(groups):
            at = choice_ref[0] ^ piece
            for number in range(groups):

                @pl.when(at == number)
                def _(piece=piece, number=number):
                    low = 0
                    for tiles in (early, late):
                        each = len(tiles) // groups
                        for k, lanes in tiles[number * each : (number + 1) * each]:
                            value = refs[piece][:, low : low + PAIR].astype(jnp.float32)
                            low += PAIR
                            if k < 3:
                                outs[k][:, lanes : lanes + PAIR] = value
                            elif lanes:
                                rows = width // members
                                for half in range(width // PAIR):
                                    part = value[half * rows : (half + 1) * rows]
                                    outs[3][:, half * PAIR : (half + 1) * PAIR] = part
                            else:
                                row = 0
                                for count_rows, out in zip(counts, outs[4:]):
                                    for start in range(0, out.shape[0], PAIR):
                                        size = min(PAIR, out.shape[0] - start)
                                        out[start : start + size] = value[row, :size]
                                        row += 1

    grad_query, grad_key, grad_value, grad_target, *small = place(
        put_last,
        last,
        [(share, model)] * 3
        + [(width // members, width)]
        + [(vector.shape[0] // members,) for vector in summed],
        (),
        group,
    )
    return (
        losses[0],
        input_grad,
        target_grad,
        grad_query,
        small[0],
        grad_key,
        grad_value,
        small[1],
        grad_out,
        small[2],
        small[3],
        small[4],
        grad_up,
        small[5],
        grad_down,
        small[6],
        small[7],
        small[8],
        grad_final,
        small[9],
        grad_target,
        small[10],
    )


def solution(mesh):
    placed = (
        P(("grp", "tm"), None),
        P(("grp", "tm"), None),
        P(("grp", "tm"), None),
        P(("grp", "tm")),
        P(("grp", "tm"), None),
        P(),
        P(),
        P(),
        P(),
        P(),
        P(),
        P(),
        P(),
        P(),
        P(),
        P(),
        P(),
        P(),
        P(),
        P(),
        P(),
        P(),
        P(),
        P(),
    )
    return jax.shard_map(
        on_device,
        mesh=mesh,
        in_specs=placed,
        out_specs=(
            P(("grp", "tm")),
            P(("grp", "tm"), None),
            P(("grp", "tm"), None),
            P("tm", None),
            P("tm"),
            P("tm", None),
            P("tm", None),
            P("tm"),
            P("tm", None),
            P("tm"),
            P("tm"),
            P("tm"),
            P("tm", None),
            P("tm"),
            P("tm", None),
            P("tm"),
            P("tm"),
            P("tm"),
            P("tm", None),
            P("tm"),
            P("tm", None),
            P("tm"),
        ),
        check_vma=False,
    )
```

time: 3960 us -> 361 us (0.09)
  waiting for transfers between devices: 2110 us -> 30.2 us
  local copies, waits for them, and re-layouts: 762 us -> 14.1 us
  matrix products: 665 us -> 0 us
  other arithmetic: 316 us -> 6.14 us
  Pallas kernels: 0 us -> 255 us
    all_to_all x3 -> x2, waiting for transfers between devices: 1130 us -> 8.3 us  [the longest x1 8.3 us: on_device(): most = lax.all_to_all(most_shares, 'grp', 0, 0, tiled=True)]
    reduce_scatter x4 -> x2, waiting for transfers between devices: 699 us -> 7.65 us  [the longest x1 7.65 us: on_device(): came = lax.psum_scatter(d_rows, 'tm', scatter_dimension=0, tiled=True)]
    dot_general x70 -> x0, matrix products: 665 us -> none  [the longest x24 198 us: product_left(): lax.dot_general(left, right, (((0,), (0,)), ((), ())), preferred_element_...]
    gather x1 -> x2, local copies, waits for them, and re-layouts: 402 us -> 1.28 us  [the longest x1 0.64 us: attention_plan(): high = (bounds[last] + chunk - 1) // chunk]
    pallas_call x0 -> x25, Pallas kernels: none -> 255 us  [the longest x3 41.8 us: attend_back(): pl.pallas_call(functools.partial(backward_kernel, width // PAIR, chunk, u...]
    unnamed x14 -> x3, waiting for transfers between devices: 241 us -> 0.05 us
    reduce_sum x53 -> x6, other arithmetic: 126 us -> 0.88 us  [total(): return jnp.sum(values, axis=0)]
    all_to_all x5 -> x0, local copies, waits for them, and re-layouts: 108 us -> none  [the longest x1 47.3 us: on_device(): came = lax.all_to_all(sent, 'tm', split_axis=1, concat_axis=1, tiled=True)]
  transfers between devices with their start and end apart: 13 -> 23, of which waited for: 10 -> 9; matrix products, arithmetic and copies ran while one was open for 17% -> 4% of each run, Pallas kernels for 0% -> 57%
where the time goes in v1:
time: 361 us; the launch traced here: 354 us
  Pallas kernels  255 us (71%)
  starting transfers between devices  34.5 us (10%)
  waiting for transfers between devices  30.2 us (8%)
  between operations  14.7 us (4%)
  local copies, waits for them, and re-layouts  14.1 us (4%)
  other arithmetic  6.14 us (2%)
    pallas_call x3, Pallas kernels, attend_back(): pl.pallas_call(functools.partial(backward_kernel, width // PAIR, chunk, u...  41.8 us
    pallas_call x1, Pallas kernels, candidates(): pl.pallas_call(functools.partial(candidate_kernel, slots, owners, keep),...  34.7 us
    pallas_call x1, Pallas kernels, feed_forward(): pl.pallas_call(functools.partial(feed_forward_kernel, max(inner // model,...  30.1 us
    pallas_call x1, Pallas kernels, attend(): pl.pallas_call(functools.partial(forward_kernel, width // PAIR, chunk, un...  25.7 us
    pallas_call x1, Pallas kernels, feed_forward_back(): pl.pallas_call(functools.partial(feed_forward_back_kernel, max(inner // m...  23.2 us
    ppermute x15, starting transfers between devices, swap(): lax.ppermute(piece, axis, [(i, i ^ k * stride) for i in range(size)])  18.9 us
    pallas_call x4, Pallas kernels, split_sum(): pl.pallas_call(functools.partial(split_kernel, [len(group) for group in s...  16.4 us
    pallas_call x1, Pallas kernels, up_grad(): pl.pallas_call(functools.partial(up_grad_kernel, groups), grid_spec=pltpu...  13.7 us
  transfers between devices with their start and end apart: 23, of which 9 were waited for; matrix products, arithmetic and copies ran while one was open for 4% of the time, Pallas kernels for 57%

profile of v1, /device:TPU:0, one launch (start us, length us, event | category | flops | bytes accessed | tf_op | source)
XLA Modules:
  0.0 354.4 jit_solution(15792460325735740186)
XLA Ops:
  7.2 3.5 shard_map.399
  10.9 9.1 %shard_map.400 = (bf16[1024,768]{1,0:T(8,128)(2,1)}, bf16[1024,768]{1,0:T(8,128)(2,1)}, bf16[1024,768]{1,0:T(8,128)(2,1)}, bf16[1024,768]{1,0:T(8,128)(2,1)}) custom-call(f32[1024,768]{1,0:T(8,128)} %frames_ref.3, f32[768,768]{1,0:T(8,128)} %refs_9_.1, f32[768,768]{1,0:T(8,128)} %refs_10_.1, f32[768,768]{1,0:T(8,128)} %refs_11_.1, f32[768]{0:T(1024)} %bq_ref.1, ...), custom_call_target="tpu_custom_call" | custom-call | flops 1 | bytes 1 | tf_op jit(solution)/shard_map/pallas_call | solution.py:853
  23.4 25.7 %shard_map.401 = (bf16[1024,768]{1,0:T(8,128)(2,1)}, f32[1024,128]{1,0:T(8,128)}, bf16[768,768]{1,0:T(8,128)(2,1)}, bf16[768,3072]{1,0:T(8,128)(2,1)}, bf16[3072...) custom-call(s32[2,4]{1,0:T(2,128)} %pad_add_fusion.span_ref, bf16[1024,768]{1,0:T(8,128)(2,1)} %get-tuple-element.113.q_ref, ...), custom_call_target="tpu_custom_call" | custom-call | flops 1 | bytes 1 | tf_op jit(solution)/shard_map/pallas_call | solution.py:147
  49.1 30.1 %shard_map.402 = (bf16[1024,768]{1,0:T(8,128)(2,1)}, f32[1024,768]{1,0:T(8,128)}, bf16[1024,3072]{1,0:T(8,128)(2,1)}, bf16[1024,3072]{1,0:T(8,128)(2,1)}, f32[10...) custom-call(bf16[1024,768]{1,0:T(8,128)(2,1)} %get-tuple-element.116, ...), custom_call_target="tpu_custom_call" | custom-call | flops 1 | bytes 1 | tf_op jit(solution)/shard_map/pallas_call | solution.py:355
  81.7 34.7 %shard_map.403 = (f32[8,1024]{1,0:T(8,128)}, bf16[1024,256]{1,0:T(8,128)(2,1)}, f32[1024,256]{1,0:T(8,128)}, bf16[8192,256]{1,0:T(8,128)(2,1)}) custom-call(s32[8,13,1024]{2,1,0:T(8,128)} %fusion.1.index_ref, bf16[8192,256]{1,0:T(8,128)(2,1)} %all-gather.2.cloned.1.call-done.rows_ref, f32[256,1024]{1,0:T(8,128)} %get-tuple-element.121.unit_ref, ...), custom_call_target="tpu_custom_call" | custom-call | flops 1 | bytes 1 | tf_op jit(solution)/shard_map/pallas_call | solution.py:547
  116.5 23.2 %shard_map.404 = (bf16[1024,768]{1,0:T(8,128)(2,1)}, bf16[1024,3072]{1,0:T(8,128)(2,1)}, f32[1024,768]{1,0:T(8,128)}, bf16[1024,768]{1,0:T(8,128)(2,1)}, bf16[10...) custom-call(bf16[1024,256]{1,0:T(8,128)(2,1)} %get-tuple-element.125.d_final_ref.final_ref, ...), custom_call_target="tpu_custom_call" | custom-call | flops 1 | bytes 1 | tf_op jit(solution)/shard_map/pallas_call | solution.py:443
  139.7 12.2 %shard_map.405.refs_0_ = bf16[8,4,192,384]{3,2,1,0:T(8,128)(2,1)} custom-call(bf16[1024,3072]{1,0:T(8,128)(2,1)} %get-tuple-element.137.active_ref, bf16[1024,768]{1,0:T(8,128)(2,1)} %get-tuple-element.138.grad_ref), custom_call_target="tpu_custom_call" | custom-call | flops 1 | bytes 1 | tf_op jit(solution)/shard_map/pallas_call | solution.py:598
  152.0 13.7 %shard_map.406 = (bf16[4,4,96,1024]{3,2,1,0:T(8,128)(2,1)}, bf16[4,4,96,1024]{3,2,1,0:T(8,128)(2,1)}) custom-call(s32[1]{0:T(128)} %bitcast.11.core_ref, bf16[1024,768]{1,0:T(8,128)(2,1)} %get-tuple-element.133.hidden_ref, bf16[1024,3072]{1,0:T(8,128)(2,1)} %get-tuple-element.134.upper_ref, bf16[1024,768]{1,0:T(8,128)(2,1)} %get-tuple-element.116.attended_ref, ...), custom_call_target="tpu_custom_call" | custom-call | flops 1 | bytes 1 | tf_op jit(solution)/shard_map/pallas_call | solution.py:653
  166.0 7.7 %reduce-scatter.3.cloned.1.call-done.came_ref = bf16[1024,256]{1,0:T(8,128)(2,1)} async-done(((bf16[8192,256]{1,0:T(8,128)(2,1)}), bf16[1024,256]{1,0:T(8,128)(2,1)}) %reduce-scatter.3.cloned.1.call-update) | async-done | bytes 524304 | tf_op jit(solution)/shard_map/reduce_scatter | solution.py:1096
  173.7 4.0 %shard_map.407 = (f32[1024,256]{1,0:T(8,128)}, f32[256,256]{1,0:T(8,128)}, f32[8,256]{1,0:T(8,128)}) custom-call(bf16[1024,256]{1,0:T(8,128)(2,1)} %reduce-scatter.3.cloned.1.call-done.came_ref, f32[1024,256]{1,0:T(8,128)} %get-tuple-element.142.part_ref, f32[1024,256]{1,0:T(8,128)} %get-tuple-element.143.unit_ref, ...), custom_call_target="tpu_custom_call" | custom-call | flops 1 | bytes 1 | tf_op jit(solution)/shard_map/pallas_call | solution.py:748
  177.7 6.0 %shard_map.408 = (bf16[4,96,1024]{2,1,0:T(8,128)(2,1)}, bf16[4,96,1024]{2,1,0:T(8,128)(2,1)}, bf16[4,96,1024]{2,1,0:T(8,128)(2,1)}, bf16[4,96,1024]{2,1,0:T(8,128)(2,1)}) custom-call(s32[1]{0:T(128)} %bitcast.10.choice_ref.refs_0_, bf16[4,4,96,1024]{3,2,1,0:T(8,128)(2,1)} %get-tuple-element.139.refs_0_, ...), custom_call_target="tpu_custom_call" | custom-call | flops 1 | bytes 1 | tf_op jit(solution)/shard_map/pallas_call | solution.py:906
  187.3 14.2 %shard_map.409 = (bf16[1024,256]{1,0:T(8,128)(2,1)}, bf16[1024,256]{1,0:T(8,128)(2,1)}, bf16[1024,256]{1,0:T(8,128)(2,1)}, f32[2,8,256]{2,1,0:T(8,128)}) custom-call(s32[2,4]{1,0:T(2,128)} %pad_add_fusion.span_ref, bf16[1024,768]{1,0:T(8,128)(2,1)} %get-tuple-element.113.q_ref, bf16[1024,768]{1,0:T(8,128)(2,1)} %get-tuple-element.114.k_ref, ...), custom_call_target="tpu_custom_call" | custom-call | flops 1 | bytes 1 | tf_op jit(solution)/shard_map/pallas_call | solution.py:217
  201.5 13.9 %shard_map.410 = (bf16[1024,256]{1,0:T(8,128)(2,1)}, bf16[1024,256]{1,0:T(8,128)(2,1)}, bf16[1024,256]{1,0:T(8,128)(2,1)}, f32[2,8,256]{2,1,0:T(8,128)}) custom-call(s32[2,4]{1,0:T(2,128)} %pad_add_fusion.span_ref, bf16[1024,768]{1,0:T(8,128)(2,1)} %get-tuple-element.113.q_ref, bf16[1024,768]{1,0:T(8,128)(2,1)} %get-tuple-element.114.k_ref, ...), custom_call_target="tpu_custom_call" | custom-call | flops 1 | bytes 1 | tf_op jit(solution)/shard_map/pallas_call | solution.py:217
  215.5 6.8 %shard_map.411 = (bf16[4,4,96,384]{3,2,1,0:T(8,128)(2,1)}, bf16[4,4,96,384]{3,2,1,0:T(8,128)(2,1)}) custom-call(s32[1]{0:T(128)} %bitcast.11.core_ref, bf16[1024,768]{1,0:T(8,128)(2,1)} %get-tuple-element.149.frames_ref, bf16[1024,256]{1,0:T(8,128)(2,1)} %get-tuple-element.147.refs_0_, bf16[1024,256]{1,0:T(8,128)(2,1)} %get-tuple-element.148.refs_1_.refs_6_, ...), custom_call_target="tpu_custom_call" | custom-call | flops 1 | bytes 1 | tf_op jit(solution)/shard_map/pallas_call | solution.py:706
  223.6 4.0 %shard_map.412.refs_3_ = bf16[4,96,1024]{2,1,0:T(8,128)(2,1)} custom-call(bf16[4,96,1024]{2,1,0:T(8,128)(2,1)} %get-tuple-element.156.refs_0_, bf16[4,96,1024]{2,1,0:T(8,128)(2,1)} %copy-done.4, bf16[4,96,1024]{2,1,0:T(8,128)(2,1)} %copy-done.5, bf16[4,96,1024]{2,1,0:T(8,128)(2,1)} %collective-permute-done.4.refs_3_, ...), custom_call_target="tpu_custom_call" | custom-call | flops 1 | bytes 1 | tf_op jit(solution)/shard_map/pallas_call | solution.py:940
  227.7 11.1 %all-to-all-start = ((bf16[4,96,1024]{2,1,0:T(8,128)(2,1)}), bf16[4,96,1024]{2,1,0:T(8,128)(2,1)S(1)}, u32[]{:S(2)}, u32[]{:S(2)}) async-start(bf16[4,96,1024]{2,1,0:T(8,128)(2,1)} %shard_map.412.refs_3_), calls=%async_computation.2 | async-start | bytes 1572864 | tf_op jit(solution)/shard_map/all_to_all | solution.py:964
  243.4 4.0 %shard_map.413 = (bf16[6,96,384]{2,1,0:T(8,128)(2,1)}, bf16[6,96,384]{2,1,0:T(8,128)(2,1)}, bf16[6,96,384]{2,1,0:T(8,128)(2,1)}, bf16[6,96,384]{2,1,0:T(8,128)(2,1)}) custom-call(s32[1]{0:T(128)} %bitcast.10.choice_ref.refs_0_, bf16[4,4,96,384]{3,2,1,0:T(8,128)(2,1)} %get-tuple-element.154.refs_0_, bf16[4,4,96,384]{3,2,1,0:T(8,128)(2,1)} %collective-permute-done.1.refs_1_, ...), custom_call_target="tpu_custom_call" | custom-call | flops 1 | bytes 1 | tf_op jit(solution)/shard_map/pallas_call | solution.py:906
  251.4 13.7 %shard_map.414 = (bf16[1024,256]{1,0:T(8,128)(2,1)}, bf16[1024,256]{1,0:T(8,128)(2,1)}, bf16[1024,256]{1,0:T(8,128)(2,1)}, f32[2,8,256]{2,1,0:T(8,128)}) custom-call(s32[2,4]{1,0:T(2,128)} %pad_add_fusion.span_ref, bf16[1024,768]{1,0:T(8,128)(2,1)} %get-tuple-element.113.q_ref, bf16[1024,768]{1,0:T(8,128)(2,1)} %get-tuple-element.114.k_ref, ...), custom_call_target="tpu_custom_call" | custom-call | flops 1 | bytes 1 | tf_op jit(solution)/shard_map/pallas_call | solution.py:217
  271.4 4.5 %shard_map.415.done_ref.refs_0_ = bf16[6,96,384]{2,1,0:T(8,128)(2,1)} custom-call(bf16[6,96,384]{2,1,0:T(8,128)(2,1)} %get-tuple-element.169.refs_0_, bf16[6,96,384]{2,1,0:T(8,128)(2,1)} %copy-done.6, bf16[6,96,384]{2,1,0:T(8,128)(2,1)} %copy-done.7, bf16[6,96,384]{2,1,0:T(8,128)(2,1)} %collective-permute-done.7.refs_3_, ...), custom_call_target="tpu_custom_call" | custom-call | flops 1 | bytes 1 | tf_op jit(solution)/shard_map/pallas_call | solution.py:940
  279.3 3.9 %all-to-all-start.1 = ((bf16[4,96,1792]{2,1,0:T(8,128)(2,1)}), bf16[4,96,1792]{2,1,0:T(8,128)(2,1)S(1)}, u32[]{:S(2)}, u32[]{:S(2)}) async-start(bf16[4,96,1792]{2,1,0:T(8,128)(2,1)} %shard_map.416.refs_4_), calls=%async_computation.3 | async-start | bytes 2752512 | tf_op jit(solution)/shard_map/all_to_all | solution.py:1232
  284.4 4.7 %shard_map.417 = (bf16[4,4,96,256]{3,2,1,0:T(8,128)(2,1)}, bf16[4,4,96,256]{3,2,1,0:T(8,128)(2,1)}) custom-call(s32[1]{0:T(128)} %bitcast.11.core_ref, bf16[1024,768]{1,0:T(8,128)(2,1)} %get-tuple-element.149.frames_ref, bf16[1024,256]{1,0:T(8,128)(2,1)} %get-tuple-element.160.refs_4_.refs_0_.refs_2_, bf16[1024,256]{1,0:T(8,128)(2,1)} %get-tuple-element.161.refs_1_.refs_5_, ...), custom_call_target="tpu_custom_call" | custom-call | flops 1 | bytes 1 | tf_op jit(solution)/shard_map/pallas_call | solution.py:706
  291.8 8.3 %all-to-all-done.1.refs_2_.refs_0_ = bf16[4,96,1792]{2,1,0:T(8,128)(2,1)S(1)} async-done(((bf16[4,96,1792]{2,1,0:T(8,128)(2,1)}), bf16[4,96,1792]{2,1,0:T(8,128)(2,1)S(1)}, u32[]{:S(2)}, u32[]{:S(2)}) %all-to-all-start.1) | async-done | bytes 1376288 | tf_op jit(solution)/shard_map/all_to_all | solution.py:1232
  308.0 10.5 %shard_map.419.refs_5_ = f32[1024,768]{1,0:T(8,128)} custom-call(f32[1024,768]{1,0:T(8,128)} %get-tuple-element.130.resid_ref, bf16[1024,256]{1,0:T(8,128)(2,1)} %get-tuple-element.147.refs_0_, bf16[1024,256]{1,0:T(8,128)(2,1)} %get-tuple-element.148.refs_1_.refs_6_, bf16[1024,256]{1,0:T(8,128)(2,1)} %get-tuple-element.160.refs_4_.refs_0_.refs_2_, ...), custom_call_target="tpu_custom_call" | custom-call | flops 1 | bytes 1 | tf_op jit(solution)/shard_map/pallas_call | solution.py:785
  330.1 5.2 %collective-permute-done.13.refs_2_ = bf16[96,640]{1,0:T(8,128)(2,1)S(1)} collective-permute-done((bf16[96,640]{1,0:T(8,128)(2,1)}, bf16[96,640]{1,0:T(8,128)(2,1)S(1)}, u32[]{:S(2)}, u32[]{:S(2)}) %collective-permute-start.13) | collective-permute-done | bytes 122912 | tf_op jit(solution)/shard_map/ppermute | solution.py:924
  (186 shorter events, 64.8 us)
Async XLA Ops:
  7.2 74.5 %all-gather.2.cloned.1.call-start = ((), (), s32[]{:S(2)}) async-start(), calls=%async_computation.4 | async-start | bytes 4718592 | tf_op jit(solution)/shard_map/all_gather | solution.py:1061
  10.8 162.9 %reduce-scatter.3.cloned.1.call-start = ((), (), s32[]{:S(2)}) async-start(), calls=%async_computation.5 | async-start | bytes 4718592 | tf_op jit(solution)/shard_map/reduce_scatter | solution.py:1096
  49.1 30.1 %copy-start.8 = (s32[1024,100]{0,1:T(8,128)S(1)}, s32[1024,100]{0,1:T(8,128)}, u32[]{:S(2)}) copy-start(s32[1024,100]{0,1:T(8,128)} %param.28) | copy-start | bytes 1228804
  116.4 127.0 %reduce-scatter.5.cloned.1.call-start = ((), (), s32[]{:S(2)}) async-start(), calls=%async_computation.6 | async-start | bytes 5308416 | tf_op jit(solution)/shard_map/reduce_scatter | solution.py:960
  165.6 12.1 %collective-permute-start = (bf16[4,4,96,1024]{3,2,1,0:T(8,128)(2,1)}, bf16[4,4,96,1024]{3,2,1,0:T(8,128)(2,1)}, u32[]{:S(2)}, u32[]{:S(2)}) collective-permute-start(bf16[4,4,96,1024]{3,2,1,0:T(8,128)(2,1)} %get-tuple-element.140.refs_0_), channel_id=1, source_target_pairs={{0,1},{1,0},{2,3},{3,2},{4,5},{5,4},{6,7},{7,6},{8,9},{9,8},{10,11... | collective-permute-start | bytes 9437192 | tf_op jit(solution)/shard_map/ppermute | solution.py:870
  183.7 38.8 %collective-permute-start.2 = (bf16[4,96,1024]{2,1,0:T(8,128)(2,1)}, bf16[4,96,1024]{2,1,0:T(8,128)(2,1)S(1)}, u32[]{:S(2)}, u32[]{:S(2)}) collective-permute-start(bf16[4,96,1024]{2,1,0:T(8,128)(2,1)} %get-tuple-element.146.refs_0_), channel_id=1, source_target_pairs={{0,8},{8,0},{16,24},{24,16},{1,9},{9,1},{17,25},{25,17},{2,10},{10... | collective-permute-start | bytes 2359304 | tf_op jit(solution)/shard_map/ppermute | solution.py:924
  185.4 37.1 %collective-permute-start.3 = (bf16[4,96,1024]{2,1,0:T(8,128)(2,1)}, bf16[4,96,1024]{2,1,0:T(8,128)(2,1)S(1)}, u32[]{:S(2)}, u32[]{:S(2)}) collective-permute-start(bf16[4,96,1024]{2,1,0:T(8,128)(2,1)} %get-tuple-element.157), channel_id=1, source_target_pairs={{0,16},{8,24},{16,0},{24,8},{1,17},{9,25},{17,1},{25,9},{2,18},{10... | collective-permute-start | bytes 2359304 | tf_op jit(solution)/shard_map/ppermute | solution.py:924
  187.3 35.2 %collective-permute-start.4 = (bf16[4,96,1024]{2,1,0:T(8,128)(2,1)}, bf16[4,96,1024]{2,1,0:T(8,128)(2,1)}, u32[]{:S(2)}, u32[]{:S(2)}) collective-permute-start(bf16[4,96,1024]{2,1,0:T(8,128)(2,1)} %get-tuple-element.158), channel_id=1, source_target_pairs={{0,24},{8,16},{16,8},{24,0},{1,25},{9,17},{17,9},{25,1},{2,26},{10... | collective-permute-start | bytes 2359304 | tf_op jit(solution)/shard_map/ppermute | solution.py:924
  222.3 21.2 %collective-permute-start.1 = (bf16[4,4,96,384]{3,2,1,0:T(8,128)(2,1)}, bf16[4,4,96,384]{3,2,1,0:T(8,128)(2,1)}, u32[]{:S(2)}, u32[]{:S(2)}) collective-permute-start(bf16[4,4,96,384]{3,2,1,0:T(8,128)(2,1)} %get-tuple-element.155.refs_4_), channel_id=1, source_target_pairs={{0,1},{1,0},{2,3},{3,2},{4,5},{5,4},{6,7},{7,6},{8,9},{9,8},{10,11... | collective-permute-start | bytes 3538952 | tf_op jit(solution)/shard_map/ppermute | solution.py:870
  227.7 48.3 %all-to-all-start = ((bf16[4,96,1024]{2,1,0:T(8,128)(2,1)}), bf16[4,96,1024]{2,1,0:T(8,128)(2,1)S(1)}, u32[]{:S(2)}, u32[]{:S(2)}) async-start(bf16[4,96,1024]{2,1,0:T(8,128)(2,1)} %shard_map.412.refs_3_), calls=%async_computation.2 | async-start | bytes 1572864 | tf_op jit(solution)/shard_map/all_to_all | solution.py:964
  247.4 19.7 %collective-permute-start.5 = (bf16[6,96,384]{2,1,0:T(8,128)(2,1)}, bf16[6,96,384]{2,1,0:T(8,128)(2,1)S(1)}, u32[]{:S(2)}, u32[]{:S(2)}) collective-permute-start(bf16[6,96,384]{2,1,0:T(8,128)(2,1)} %get-tuple-element.159.refs_0_), channel_id=1, source_target_pairs={{0,8},{8,0},{16,24},{24,16},{1,9},{9,1},{17,25},{25,17},{2,10},{10... | collective-permute-start | bytes 1327112 | tf_op jit(solution)/shard_map/ppermute | solution.py:924
  247.4 22.2 %collective-permute-start.6 = (bf16[6,96,384]{2,1,0:T(8,128)(2,1)}, bf16[6,96,384]{2,1,0:T(8,128)(2,1)S(1)}, u32[]{:S(2)}, u32[]{:S(2)}) collective-permute-start(bf16[6,96,384]{2,1,0:T(8,128)(2,1)} %get-tuple-element.170), channel_id=1, source_target_pairs={{0,16},{8,24},{16,0},{24,8},{1,17},{9,25},{17,1},{25,9},{2,18},{10... | collective-permute-start | bytes 1327112 | tf_op jit(solution)/shard_map/ppermute | solution.py:924
  250.0 21.4 %collective-permute-start.7 = (bf16[6,96,384]{2,1,0:T(8,128)(2,1)}, bf16[6,96,384]{2,1,0:T(8,128)(2,1)}, u32[]{:S(2)}, u32[]{:S(2)}) collective-permute-start(bf16[6,96,384]{2,1,0:T(8,128)(2,1)} %get-tuple-element.171), channel_id=1, source_target_pairs={{0,24},{8,16},{16,8},{24,0},{1,25},{9,17},{17,9},{25,1},{2,26},{10... | collective-permute-start | bytes 1327112 | tf_op jit(solution)/shard_map/ppermute | solution.py:924
  279.3 20.7 %all-to-all-start.1 = ((bf16[4,96,1792]{2,1,0:T(8,128)(2,1)}), bf16[4,96,1792]{2,1,0:T(8,128)(2,1)S(1)}, u32[]{:S(2)}, u32[]{:S(2)}) async-start(bf16[4,96,1792]{2,1,0:T(8,128)(2,1)} %shard_map.416.refs_4_), calls=%async_computation.3 | async-start | bytes 2752512 | tf_op jit(solution)/shard_map/all_to_all | solution.py:1232
  289.2 2.6 collective-permute-start.8
  304.5 14.0 %collective-permute-start.9 = (bf16[4,96,256]{2,1,0:T(8,128)(2,1)}, bf16[4,96,256]{2,1,0:T(8,128)(2,1)S(1)}, u32[]{:S(2)}, u32[]{:S(2)}) collective-permute-start(bf16[4,96,256]{2,1,0:T(8,128)(2,1)} %get-tuple-element.174.refs_12_), channel_id=1, source_target_pairs={{0,8},{8,0},{16,24},{24,16},{1,9},{9,1},{17,25},{25,17},{2,10},{10... | collective-permute-start | bytes 589832 | tf_op jit(solution)/shard_map/ppermute | solution.py:924
  306.0 12.6 %collective-permute-start.10 = (bf16[4,96,256]{2,1,0:T(8,128)(2,1)}, bf16[4,96,256]{2,1,0:T(8,128)(2,1)S(1)}, u32[]{:S(2)}, u32[]{:S(2)}) collective-permute-start(bf16[4,96,256]{2,1,0:T(8,128)(2,1)} %get-tuple-element.177), channel_id=1, source_target_pairs={{0,16},{8,24},{16,0},{24,8},{1,17},{9,25},{17,1},{25,9},{2,18},{10... | collective-permute-start | bytes 589832 | tf_op jit(solution)/shard_map/ppermute | solution.py:924
  306.5 12.0 %collective-permute-start.11 = (bf16[4,96,256]{2,1,0:T(8,128)(2,1)}, bf16[4,96,256]{2,1,0:T(8,128)(2,1)S(1)}, u32[]{:S(2)}, u32[]{:S(2)}) collective-permute-start(bf16[4,96,256]{2,1,0:T(8,128)(2,1)} %get-tuple-element.178), channel_id=1, source_target_pairs={{0,24},{8,16},{16,8},{24,0},{1,25},{9,17},{17,9},{25,1},{2,26},{10... | collective-permute-start | bytes 589832 | tf_op jit(solution)/shard_map/ppermute | solution.py:924
  322.3 7.7 %collective-permute-start.12 = (bf16[96,640]{1,0:T(8,128)(2,1)}, bf16[96,640]{1,0:T(8,128)(2,1)S(1)}, u32[]{:S(2)}, u32[]{:S(2)}) collective-permute-start(bf16[96,640]{1,0:T(8,128)(2,1)} %get-tuple-element.180.refs_1_), channel_id=1, source_target_pairs={{0,2},{1,3},{2,0},{3,1},{4,6},{5,7},{6,4},{7,5},{8,10},{9,11},{10,... | collective-permute-start | bytes 368648 | tf_op jit(solution)/shard_map/ppermute | solution.py:924
  324.0 11.2 %collective-permute-start.13 = (bf16[96,640]{1,0:T(8,128)(2,1)}, bf16[96,640]{1,0:T(8,128)(2,1)S(1)}, u32[]{:S(2)}, u32[]{:S(2)}) collective-permute-start(bf16[96,640]{1,0:T(8,128)(2,1)} %get-tuple-element.181), channel_id=1, source_target_pairs={{0,4},{1,5},{2,6},{3,7},{4,0},{5,1},{6,2},{7,3},{8,12},{9,13},{10,... | collective-permute-start | bytes 368648 | tf_op jit(solution)/shard_map/ppermute | solution.py:924
  326.4 8.8 %collective-permute-start.14 = (bf16[96,640]{1,0:T(8,128)(2,1)}, bf16[96,640]{1,0:T(8,128)(2,1)S(1)}, u32[]{:S(2)}, u32[]{:S(2)}) collective-permute-start(bf16[96,640]{1,0:T(8,128)(2,1)} %get-tuple-element.182), channel_id=1, source_target_pairs={{0,6},{1,7},{2,4},{3,5},{4,2},{5,3},{6,0},{7,1},{8,14},{9,15},{10,... | collective-permute-start | bytes 368648 | tf_op jit(solution)/shard_map/ppermute | solution.py:924
  337.7 5.1 %collective-permute-start.15 = (bf16[96,640]{1,0:T(8,128)(2,1)}, bf16[96,640]{1,0:T(8,128)(2,1)S(1)}, u32[]{:S(2)}, u32[]{:S(2)}) collective-permute-start(bf16[96,640]{1,0:T(8,128)(2,1)} %shard_map.422.refs_1_), channel_id=1, source_target_pairs={{0,8},{8,0},{16,24},{24,16},{1,9},{9,1},{17,25},{25,17},{2,10},{10... | collective-permute-start | bytes 368648 | tf_op jit(solution)/shard_map/ppermute | solution.py:924
  338.1 5.1 %collective-permute-start.16 = (bf16[96,640]{1,0:T(8,128)(2,1)}, bf16[96,640]{1,0:T(8,128)(2,1)S(1)}, u32[]{:S(2)}, u32[]{:S(2)}) collective-permute-start(bf16[96,640]{1,0:T(8,128)(2,1)} %shard_map.422.refs_1_), channel_id=1, source_target_pairs={{0,16},{8,24},{16,0},{24,8},{1,17},{9,25},{17,1},{25,9},{2,18},{10... | collective-permute-start | bytes 368648 | tf_op jit(solution)/shard_map/ppermute | solution.py:924
  338.6 6.0 %collective-permute-start.17 = (bf16[96,640]{1,0:T(8,128)(2,1)}, bf16[96,640]{1,0:T(8,128)(2,1)S(1)}, u32[]{:S(2)}, u32[]{:S(2)}) collective-permute-start(bf16[96,640]{1,0:T(8,128)(2,1)} %shard_map.422.refs_1_), channel_id=1, source_target_pairs={{0,24},{8,16},{16,8},{24,0},{1,25},{9,17},{17,9},{25,1},{2,26},{10... | collective-permute-start | bytes 368648 | tf_op jit(solution)/shard_map/ppermute | solution.py:924
  (32 other events, 180.6 us)
Sparse Core Ops, SparseCore 0:
  10.9 49.8 all-gather.1
  116.6 57.0 reduce-scatter.2
  176.0 53.0 reduce-scatter.4
